TPU v7x, 32 devices: a whole 2x2x4 slice. The times are simulated.
32 devices in a mesh: section: 2 (over core), dp: 16 (over z, y, x).
Axes of the slice: x: 2, y: 2, z: 4, core: 2. Of those that a mesh axis runs over, the one named last changes fastest.
Arguments:
- inputs: bfloat16 [6, 8192, 384], P(None, 'dp'), may hold values from -120 to 120
- series_id: int32 [6, 8192], P(None, 'dp'), may hold values from 0 to 63, as said below
- item_offset: int32 [6, 8192], P(None, 'dp'), may hold values from 0 to 383, as said below
- variate_offset: int32 [6, 8192], P(None, 'dp'), may hold values from 0 to 511, as said below
- cotangent: bfloat16 [6, 8192, 384], P(None, 'dp'), may hold values from -30 to 30
- attention_gain: bfloat16 [2, 384], P('section'), may hold values from 0.099609375 to 1.8984375
- query_weight: bfloat16 [2, 384, 384], P('section'), may hold values from -0.3125 to 0.3125
- key_weight: bfloat16 [2, 384, 384], P('section'), may hold values from -0.3125 to 0.3125
- value_weight: bfloat16 [2, 384, 384], P('section'), may hold values from -0.3125 to 0.3125
- out_weight: bfloat16 [2, 384, 384], P('section'), may hold values from -1.25 to 1.25
- variate_bias: bfloat16 [2, 6, 2], P('section'), may hold values from -3 to 3
- feed_gain: bfloat16 [2, 384], P('section'), may hold values from 0.099609375 to 1.8984375
- gate_weight: bfloat16 [2, 384, 1024], P('section'), may hold values from -0.3125 to 0.3125
- up_weight: bfloat16 [2, 384, 1024], P('section'), may hold values from -0.3125 to 0.3125
- down_weight: bfloat16 [2, 1024, 384], P('section'), may hold values from -0.1875 to 0.1875
Outputs:
- section_output: bfloat16 [2, 6, 8192, 384], P('section', None, 'dp')
- input_grads: float32 [2, 6, 8192, 384], P('section', None, 'dp')
- grad_attention_gain: float32 [2, 384], P('section')
- grad_query: float32 [2, 384, 384], P('section')
- grad_key: float32 [2, 384, 384], P('section')
- grad_value: float32 [2, 384, 384], P('section')
- grad_out: float32 [2, 384, 384], P('section')
- grad_bias: float32 [2, 6, 2], P('section')
- grad_feed_gain: float32 [2, 384], P('section')
- grad_gate: float32 [2, 384, 1024], P('section')
- grad_up: float32 [2, 384, 1024], P('section')
- grad_down: float32 [2, 1024, 384], P('section')
Inputs may be any that keep to these rules, and one draw needn't show every extreme that they name: `series_id`: tokens of one variate share a series; in each micro-batch one series, drawn from the seed, holds the first variate of every block of 512 tokens. Each aligned block of 512 tokens holds two items, runs of tokens; the first begins at 0, so a token's item_offset is at most its position in the block. Variates are runs within an item; a token's variate_offset lies between its item_offset and its position in the block.
All inputs are finite; a program needn't handle non-finite values.
Results may differ from a plain program's by a relative error of at most 0.015.
Values may be sent and summed in bfloat16 or wider, within the bound.
No kernel may reach another device: no remote copies, remote signals or barrier semaphores. Data moves between devices by JAX's collectives and lax.ppermute only.
A program may use at most 320 MiB of HBM per device.

v0:
```python
import jax
import jax.numpy as jnp
from jax import lax
from jax.sharding import PartitionSpec as P

HD = 64
BLOCK = 512
SER_DEV = 4


norm_epsilon = 1e-05
scale_epsilon = 1e-05
masked_score = -1e30
highest = lax.Precision.HIGHEST


def from_behind(x, axis, by):
    length = lax.axis_size(axis)
    pairs = [(i, i + by) for i in range(length) if 0 <= i + by < length]
    return lax.ppermute(x, axis, pairs)


def matmul(left, right):
    return jnp.dot(left, right, preferred_element_type=jnp.float32)


def matmul_left(left, right):
    return lax.dot_general(
        left, right, (((0,), (0,)), ((), ())), preferred_element_type=jnp.float32
    )


def matmul_right(left, right):
    return lax.dot_general(
        left, right, (((1,), (1,)), ((), ())), preferred_element_type=jnp.float32
    )


def rms_forward(hidden, gains):
    inverse = lax.rsqrt(jnp.mean(hidden * hidden, axis=-1, keepdims=True) + norm_epsilon)
    return (hidden * inverse * gains, inverse)


def rms_backward(hidden, inverse, gains, upstream):
    scaled = upstream * gains
    gain_grad = jnp.sum(upstream * hidden * inverse, axis=0)
    hidden_grad = inverse * scaled - hidden * inverse**3 * jnp.mean(
        scaled * hidden, axis=-1, keepdims=True
    )
    return (hidden_grad, gain_grad)


def rotary(time_rows, head_size):
    half_size = head_size // 2
    frequency = 10000.0 ** (-jnp.arange(half_size, dtype=jnp.float32) * (2.0 / head_size))
    angles = time_rows.astype(jnp.float32)[:, None] * frequency[None, :]
    return (jnp.cos(angles), jnp.sin(angles))


def turn(values, cosine, sine_part, orientation):
    half_size = values.shape[-1] // 2
    lower_half = values[..., :half_size]
    upper_half = values[..., half_size:]
    cosine = cosine[:, None, :]
    sine_part = sine_part[:, None, :] * orientation
    return jnp.concatenate(
        [
            lower_half * cosine - upper_half * sine_part,
            upper_half * cosine + lower_half * sine_part,
        ],
        axis=-1,
    )


def score_block(queries, key_rows, same_item, same_variate, variate_bias):
    scaling = queries.shape[-1] ** (-0.5)
    scores = (
        jnp.einsum("bqhe,bkhe->bhqk", queries, key_rows, preferred_element_type=jnp.float32)
        * scaling
    )
    bias_term = jnp.where(
        same_variate[:, None],
        variate_bias[:, 0][None, :, None, None],
        variate_bias[:, 1][None, :, None, None],
    )
    return jnp.where(same_item[:, None], scores + bias_term, masked_score)


def attention_forward(queries, key_rows, value_rows, same_item, same_variate, variate_bias):
    scores = score_block(queries, key_rows, same_item, same_variate, variate_bias)
    peak_score = jnp.max(scores, axis=-1, keepdims=True)
    exponent = jnp.exp(scores - peak_score)
    total_sum = jnp.sum(exponent, axis=-1, keepdims=True)
    softmax_low = (exponent / total_sum).astype(jnp.bfloat16)
    attended = jnp.einsum(
        "bhqk,bkhe->bqhe", softmax_low, value_rows, preferred_element_type=jnp.float32
    )
    return (attended, peak_score + jnp.log(total_sum))


def attention_backward(
    queries, key_rows, value_rows, same_item, same_variate, variate_bias, log_total, attended_grad
):
    scores = score_block(queries, key_rows, same_item, same_variate, variate_bias)
    softmax = jnp.exp(scores - log_total)
    softmax_low = softmax.astype(jnp.bfloat16)
    softmax_grad = jnp.einsum(
        "bqhe,bkhe->bhqk", attended_grad, value_rows, preferred_element_type=jnp.float32
    )
    value_grad = jnp.einsum(
        "bhqk,bqhe->bkhe", softmax_low, attended_grad, preferred_element_type=jnp.float32
    )
    inner_sum = jnp.sum(softmax_grad * softmax, axis=-1, keepdims=True)
    score_grad = jnp.where(same_item[:, None], softmax * (softmax_grad - inner_sum), 0.0).astype(
        jnp.bfloat16
    )
    scaling = queries.shape[-1] ** (-0.5)
    query_grad = (
        jnp.einsum("bhqk,bkhe->bqhe", score_grad, key_rows, preferred_element_type=jnp.float32)
        * scaling
    )
    key_grad = (
        jnp.einsum("bhqk,bqhe->bkhe", score_grad, queries, preferred_element_type=jnp.float32)
        * scaling
    )
    same_sum = jnp.sum(
        jnp.where(same_variate[:, None], score_grad, 0.0), axis=(0, 2, 3), dtype=jnp.float32
    )
    other_sum = jnp.sum(
        jnp.where(same_variate[:, None], 0.0, score_grad), axis=(0, 2, 3), dtype=jnp.float32
    )
    return (query_grad, key_grad, value_grad, jnp.stack([same_sum, other_sum], axis=-1))


def layer_forward(layer_in, geometry, params):
    cosine, sine_part, same_item, same_variate = geometry
    (
        attention_gain,
        query_weight,
        key_weight,
        value_weight,
        out_weight,
        variate_bias,
        feed_gain,
        gate_weight,
        up_weight,
        down_weight,
    ) = params
    row_count, model_width = layer_in.shape
    head_count = variate_bias.shape[0]
    head_size = model_width // head_count
    block_count = row_count // BLOCK
    normed, inverse_one = rms_forward(layer_in, attention_gain)
    normed_low = normed.astype(jnp.bfloat16)

    def by_blocks(array):
        return array.astype(jnp.bfloat16).reshape(block_count, BLOCK, head_count, head_size)

    queries = by_blocks(
        turn(
            matmul(normed_low, query_weight).reshape(row_count, head_count, head_size),
            cosine,
            sine_part,
            1.0,
        )
    )
    key_rows = by_blocks(
        turn(
            matmul(normed_low, key_weight).reshape(row_count, head_count, head_size),
            cosine,
            sine_part,
            1.0,
        )
    )
    value_rows = by_blocks(matmul(normed_low, value_weight))
    attended, log_total = attention_forward(
        queries, key_rows, value_rows, same_item, same_variate, variate_bias
    )
    mixed_low = attended.reshape(row_count, model_width).astype(jnp.bfloat16)
    middle = layer_in + matmul(mixed_low, out_weight)
    normed_feed, inverse_two = rms_forward(middle, feed_gain)
    feed_low = normed_feed.astype(jnp.bfloat16)
    gate_part = matmul(feed_low, gate_weight)
    up_part = matmul(feed_low, up_weight)
    activated = (jax.nn.silu(gate_part) * up_part).astype(jnp.bfloat16)
    result = (middle + matmul(activated, down_weight)).astype(jnp.bfloat16)
    kept = (
        layer_in,
        inverse_one,
        normed_low,
        queries,
        key_rows,
        value_rows,
        log_total,
        mixed_low,
        middle,
        inverse_two,
        feed_low,
        gate_part,
        up_part,
        activated,
    )
    return (result, kept)


def feed_backward(grad_low, kept, params):
    (
        layer_in,
        inverse_one,
        normed_low,
        queries,
        key_rows,
        value_rows,
        log_total,
        mixed_low,
        middle,
        inverse_two,
        feed_low,
        gate_part,
        up_part,
        activated,
    ) = kept
    feed_gain, gate_weight, up_weight, down_weight = (params[6], params[7], params[8], params[9])
    hidden_grad = matmul_right(grad_low, down_weight)
    down_grad = matmul_left(activated, grad_low)
    sigmoid = jax.nn.sigmoid(gate_part)
    swish = gate_part * sigmoid
    gate_grad = (hidden_grad * up_part * (sigmoid + swish * (1.0 - sigmoid))).astype(jnp.bfloat16)
    up_grad = (hidden_grad * swish).astype(jnp.bfloat16)
    normed_grad = matmul_right(gate_grad, gate_weight) + matmul_right(up_grad, up_weight)
    branch_grad, feed_gain_grad = rms_backward(middle, inverse_two, feed_gain, normed_grad)
    middle_grad = grad_low.astype(jnp.float32) + branch_grad
    return (
        middle_grad,
        (
            feed_gain_grad,
            matmul_left(feed_low, gate_grad),
            matmul_left(feed_low, up_grad),
            down_grad,
        ),
    )


def attention_backward_part(middle_grad, kept, geometry, params):
    (
        layer_in,
        inverse_one,
        normed_low,
        queries,
        key_rows,
        value_rows,
        log_total,
        mixed_low,
        middle,
        inverse_two,
        feed_low,
        gate_part,
        up_part,
        activated,
    ) = kept
    cosine, sine_part, same_item, same_variate = geometry
    attention_gain, query_weight, key_weight, value_weight, out_weight, variate_bias = params[:6]
    row_count, model_width = middle_grad.shape
    block_count, block_rows, head_count, head_size = queries.shape
    mix_grad = middle_grad.astype(jnp.bfloat16)
    out_grad = matmul_left(mixed_low, mix_grad)
    attended_grad = (
        matmul_right(mix_grad, out_weight)
        .astype(jnp.bfloat16)
        .reshape(block_count, block_rows, head_count, head_size)
    )
    query_grad, key_grad, value_grad, bias_grad = attention_backward(
        queries,
        key_rows,
        value_rows,
        same_item,
        same_variate,
        variate_bias,
        log_total,
        attended_grad,
    )

    def by_heads(array):
        return array.reshape(row_count, head_count, head_size)

    query_low = (
        turn(by_heads(query_grad), cosine, sine_part, -1.0)
        .reshape(row_count, model_width)
        .astype(jnp.bfloat16)
    )
    key_low = (
        turn(by_heads(key_grad), cosine, sine_part, -1.0)
        .reshape(row_count, model_width)
        .astype(jnp.bfloat16)
    )
    value_low = value_grad.reshape(row_count, model_width).astype(jnp.bfloat16)
    normed_grad = (
        matmul_right(query_low, query_weight)
        + matmul_right(key_low, key_weight)
        + matmul_right(value_low, value_weight)
    )
    branch_grad, gain_grad = rms_backward(layer_in, inverse_one, attention_gain, normed_grad)
    grads = (
        gain_grad,
        matmul_left(normed_low, query_low),
        matmul_left(normed_low, key_low),
        matmul_left(normed_low, value_low),
        out_grad,
        bias_grad,
    )
    return (middle_grad + branch_grad, grads)


def series_sum(one_hot, per_row):
    return jnp.einsum("mrs,mr->ms", one_hot, per_row, precision=highest)


def series_rows(one_hot, per_series):
    return jnp.einsum("mrs,ms->mr", one_hot, per_series, precision=highest)


def standardize(inputs, one_hot, model_width):
    values = inputs.astype(jnp.float32)
    counts_here = jnp.sum(one_hot, axis=1)
    totals_here = series_sum(one_hot, jnp.sum(values, axis=-1))
    counts, series_totals = lax.psum((counts_here, totals_here), "dp")
    entries = jnp.maximum(counts, 1.0) * model_width
    centre = series_totals / entries
    centred = values - series_rows(one_hot, centre)[..., None]
    spread = lax.psum(series_sum(one_hot, jnp.sum(centred * centred, axis=-1)), "dp")
    scaling = jnp.sqrt(spread / entries + scale_epsilon)
    scaling_rows = series_rows(one_hot, scaling)[..., None]
    return (centred / scaling_rows, centred, entries, scaling, scaling_rows)


def standardize_backward(upstream, one_hot, centred, entries, scaling, scaling_rows):
    cross_sum = lax.psum(series_sum(one_hot, jnp.sum(upstream * centred, axis=-1)), "dp")
    spread_grad = -cross_sum / (2.0 * scaling**3 * entries)
    centred_grad = (
        upstream / scaling_rows + 2.0 * centred * series_rows(one_hot, spread_grad)[..., None]
    )
    mean_grad = lax.psum(series_sum(one_hot, jnp.sum(centred_grad, axis=-1)), "dp")
    return centred_grad - series_rows(one_hot, mean_grad / entries)[..., None]


def per_device(
    inputs,
    series_id,
    item_offset,
    variate_offset,
    cotangent,
    attention_gain,
    query_weight,
    key_weight,
    value_weight,
    out_weight,
    variate_bias,
    feed_gain,
    gate_weight,
    up_weight,
    down_weight,
):
    params = tuple(
        (
            weight[0]
            for weight in (
                attention_gain,
                query_weight,
                key_weight,
                value_weight,
                out_weight,
                variate_bias,
                feed_gain,
                gate_weight,
                up_weight,
                down_weight,
            )
        )
    )
    section_index = lax.axis_index("section")
    on_first = section_index == 0
    micro_count, row_count, model_width = inputs.shape
    series_count = SER_DEV * lax.axis_size("dp")
    head_size = HD
    block_count = row_count // BLOCK
    one_hot = (
        series_id[:, :, None] == jnp.arange(series_count, dtype=jnp.int32)[None, None, :]
    ).astype(jnp.float32)
    standard, centred, entries, scaling, scaling_rows = standardize(inputs, one_hot, model_width)
    position = jnp.arange(row_count, dtype=jnp.int32) % BLOCK
    time_all = position[None, :] - variate_offset
    cosine_all, sine_all = rotary(time_all.reshape(-1), head_size)
    cosine_all = cosine_all.reshape(micro_count, row_count, head_size // 2)
    sine_all = sine_all.reshape(micro_count, row_count, head_size // 2)
    item_blocks = item_offset.reshape(micro_count, block_count, BLOCK)
    variate_blocks = variate_offset.reshape(micro_count, block_count, BLOCK)
    same_item_all = item_blocks[..., :, None] == item_blocks[..., None, :]
    same_variate_all = variate_blocks[..., :, None] == variate_blocks[..., None, :]
    received = jnp.zeros((row_count, model_width), jnp.bfloat16)
    kept_steps = []
    section_rows = []
    for step_index in range(micro_count + 1):
        batch_number = jnp.where(
            on_first, min(step_index, micro_count - 1), max(step_index - 1, 0)
        ).astype(jnp.int32)
        geometry = tuple(
            (
                lax.dynamic_index_in_dim(array, batch_number, 0, keepdims=False)
                for array in (cosine_all, sine_all, same_item_all, same_variate_all)
            )
        )
        layer_in = jnp.where(
            on_first, standard[min(step_index, micro_count - 1)], received.astype(jnp.float32)
        )
        result, kept = layer_forward(layer_in, geometry, params)
        kept_steps.append((kept, geometry))
        section_rows.append(result)
        if step_index < micro_count:
            received = from_behind(result, "section", 1)
    grad_received = jnp.zeros((row_count, model_width), jnp.bfloat16)
    feed_acc = tuple((jnp.zeros(weight.shape, jnp.float32) for weight in params[6:]))
    attention_acc = tuple((jnp.zeros(weight.shape, jnp.float32) for weight in params[:6]))
    input_steps = []
    for step_index in range(micro_count + 1):
        kept, geometry = kept_steps[micro_count - step_index]
        grad_low = jnp.where(
            on_first, grad_received, cotangent[max(micro_count - 1 - step_index, 0)]
        )
        active = jnp.where(on_first, step_index >= 1, step_index < micro_count).astype(jnp.float32)
        middle_grad, feed_grads = feed_backward(grad_low, kept, params)
        feed_acc = tuple(
            (running + active * piece_grad for running, piece_grad in zip(feed_acc, feed_grads))
        )
        input_grad, attention_grads = attention_backward_part(middle_grad, kept, geometry, params)
        attention_acc = tuple(
            (
                running + active * piece_grad
                for running, piece_grad in zip(attention_acc, attention_grads)
            )
        )
        input_steps.append(input_grad)
        if step_index < micro_count:
            grad_received = from_behind(input_grad.astype(jnp.bfloat16), "section", -1)
    summed = lax.psum(
        (
            feed_acc[0],
            feed_acc[1],
            feed_acc[2],
            feed_acc[3],
            attention_acc[0],
            attention_acc[1],
            attention_acc[2],
            attention_acc[3],
            attention_acc[4],
            attention_acc[5],
        ),
        "dp",
    )
    feed_total = summed[:4]
    attention_total = summed[4:]
    second_grads = jnp.stack(
        [
            input_steps[micro_count - 1 - batch_number].astype(jnp.bfloat16).astype(jnp.float32)
            for batch_number in range(micro_count)
        ]
    )
    standard_grads = jnp.stack(
        [input_steps[micro_count - batch_number] for batch_number in range(micro_count)]
    )
    first_grads = standardize_backward(
        standard_grads, one_hot, centred, entries, scaling, scaling_rows
    )
    input_grads = jnp.where(on_first, first_grads, second_grads)[None]
    section_output = jnp.where(
        on_first, jnp.stack(section_rows[:micro_count]), jnp.stack(section_rows[1:])
    )[None]
    return (
        section_output,
        input_grads,
        attention_total[0][None],
        attention_total[1][None],
        attention_total[2][None],
        attention_total[3][None],
        attention_total[4][None],
        attention_total[5][None],
        feed_total[0][None],
        feed_total[1][None],
        feed_total[2][None],
        feed_total[3][None],
    )


def solution(mesh):
    placed = (
        P(None, "dp", None),
        P(None, "dp"),
        P(None, "dp"),
        P(None, "dp"),
        P(None, "dp", None),
        P("section", None),
        P("section", None, None),
        P("section", None, None),
        P("section", None, None),
        P("section", None, None),
        P("section", None, None),
        P("section", None),
        P("section", None, None),
        P("section", None, None),
        P("section", None, None),
    )
    return jax.shard_map(
        per_device,
        mesh=mesh,
        in_specs=placed,
        out_specs=(
            P("section", None, "dp", None),
            P("section", None, "dp", None),
            P("section", None),
            P("section", None, None),
            P("section", None, None),
            P("section", None, None),
            P("section", None, None),
            P("section", None, None),
            P("section", None),
            P("section", None, None),
            P("section", None, None),
            P("section", None, None),
        ),
        check_vma=False,
    )
```

profile of v0, /device:TPU:0, one launch (start us, length us, event | category | flops | bytes accessed | tf_op | source)
XLA Modules:
  0.0 778.1 jit_solution(2034772218918170737)
XLA Ops:
  27.9 44.0 %all-reduce.1 = (f32[6,64]{1,0:T(8,128)S(1)}, f32[6,64]{1,0:T(8,128)S(1)}) all-reduce(f32[6,64]{1,0:T(8,128)S(1)} %bitcast.1112, f32[6,64]{1,0:T(8,128)S(1)} %convert_reduce_fusion.15), channel_id=1, replica_groups=mesh['section'=2,'dp'=16] {'dp'}, use_global_device_ids=true, to_apply=%region_1.0 | all-reduce | flops 768 | bytes 6144 | tf_op jit(solution)/shard_map/psum | solution.py:326
  73.4 36.8 %psum.107 = f32[6,64]{1,0:T(8,128)S(1)} all-reduce(f32[6,64]{1,0:T(8,128)S(1)} %bitcast.1113), channel_id=1, replica_groups=mesh['section'=2,'dp'=16] {'dp'}, use_global_device_ids=true, to_apply=%region_5.0 | all-reduce | flops 384 | bytes 3072 | tf_op jit(solution)/shard_map/psum | solution.py:330
  150.9 3.4 fusion.419
  259.8 11.5 %convert_reduce_fusion.13 = (f32[6]{0:T(128)}, f32[6]{0:T(128)}, bf16[6,512,512]{1,2,0:T(8,128)(2,1)}) fusion(pred[512,512]{0,1:T(8,128)(4,1)} %get-tuple-element.164, f32[6,512,512]{1,2,0:T(8,128)} %copy-done.15, f32[6,512]{1,0:T(8,128)S(1)} %log_add_fusion.6, bf16[512,6,64]{0,2,1:T(8,128)(2,1)} %bitcast.1067, bf16[512,6,64]{0,2,1:T(8,128)(2,1)} %bitcast.1102, ...), kind=kOutput, calls=%fused_computation.20 | convolution fusion | flops 423104000 | bytes 10760240 | tf_op jit(solution)/shard_map/sub | solution.py:114
  271.3 3.3 fusion.103
  291.5 4.6 copy.232
  296.1 3.2 fusion.424
  310.0 11.5 %convert_reduce_fusion.11 = (f32[6]{0:T(128)}, f32[6]{0:T(128)}, bf16[6,512,512]{1,2,0:T(8,128)(2,1)}) fusion(pred[512,512]{0,1:T(8,128)(4,1)} %get-tuple-element.165, f32[6,512,512]{1,2,0:T(8,128)} %copy-done.14, f32[6,512]{1,0:T(8,128)S(1)} %log_add_fusion.5, bf16[512,6,64]{0,2,1:T(8,128)(2,1)} %bitcast.1069, bf16[512,6,64]{0,2,1:T(8,128)(2,1)} %bitcast.1100, ...), kind=kOutput, calls=%fused_computation.18 | convolution fusion | flops 423104000 | bytes 10760240 | tf_op jit(solution)/shard_map/sub | solution.py:114
  321.5 3.3 fusion.101
  348.9 11.2 %convert_reduce_fusion.9 = (f32[6]{0:T(128)S(1)}, f32[6]{0:T(128)S(1)}, bf16[6,512,512]{1,2,0:T(8,128)(2,1)}) fusion(pred[512,512]{0,1:T(8,128)(4,1)} %get-tuple-element.166, f32[6,512,512]{1,2,0:T(8,128)} %copy-done.13, f32[6,512]{1,0:T(8,128)S(1)} %log_add_fusion.4, bf16[512,6,64]{0,2,1:T(8,128)(2,1)} %bitcast.1071, bf16[512,6,64]{0,2,1:T(8,128)(2,1)} %bitcast.1098, ...), kind=kOutput, calls=%fused_computation.16 | convolution fusion | flops 423104000 | bytes 10760240 | tf_op jit(solution)/shard_map/sub | solution.py:114
  360.1 3.3 fusion.99
  386.4 10.7 %convert_reduce_fusion.7 = (f32[6]{0:T(128)S(1)}, f32[6]{0:T(128)S(1)}, bf16[6,512,512]{1,2,0:T(8,128)(2,1)}) fusion(pred[512,512]{0,1:T(8,128)(4,1)} %get-tuple-element.167, f32[6,512,512]{1,2,0:T(8,128)} %copy-done.12, f32[6,512]{1,0:T(8,128)S(1)} %log_add_fusion.3, bf16[512,6,64]{0,2,1:T(8,128)(2,1)S(1)} %bitcast.1073, ...), kind=kOutput, calls=%fused_computation.14 | convolution fusion | flops 423104000 | bytes 10760240 | tf_op jit(solution)/shard_map/sub | solution.py:114
  397.1 3.3 fusion.97
  423.8 10.6 %convert_reduce_fusion.5 = (f32[6]{0:T(128)S(1)}, f32[6]{0:T(128)S(1)}, bf16[6,512,512]{1,2,0:T(8,128)(2,1)}) fusion(pred[512,512]{0,1:T(8,128)(4,1)} %get-tuple-element.168, f32[6,512,512]{1,2,0:T(8,128)} %copy-done.11, f32[6,512]{1,0:T(8,128)S(1)} %copy-done.352, bf16[512,6,64]{0,2,1:T(8,128)(2,1)S(1)} %bitcast.1075, bf16[512,6,64]{0,2,1:T(8,128)(2,1)} %bitcast.1094, ...), kind=kOutput, calls=%fused_computation.12 | convolution fusion | flops 423104000 | bytes 10760240 | tf_op jit(solution)/shard_map/sub | solution.py:114
  434.5 3.3 fusion.95
  460.9 10.9 %convert_reduce_fusion.3 = (f32[6]{0:T(128)S(1)}, f32[6]{0:T(128)S(1)}, bf16[6,512,512]{1,2,0:T(8,128)(2,1)}) fusion(pred[512,512]{0,1:T(8,128)(4,1)} %copy-done.327, f32[6,512,512]{1,2,0:T(8,128)} %copy-done.10, f32[6,512]{1,0:T(8,128)S(1)} %copy-done.351, bf16[512,6,64]{0,2,1:T(8,128)(2,1)S(1)} %bitcast.1077, bf16[512,6,64]{0,2,1:T(8,128)(2,1)} %bitcast.1092, ...), kind=kOutput, calls=%fused_computation.10 | convolution fusion | flops 423104000 | bytes 10760240 | tf_op jit(solution)/shard_map/sub | solution.py:114
  471.8 3.3 fusion.93
  495.6 10.9 %convert_reduce_fusion.1 = (f32[6]{0:T(128)S(1)}, f32[6]{0:T(128)S(1)}, bf16[6,512,512]{1,2,0:T(8,128)(2,1)}) fusion(pred[512,512]{0,1:T(8,128)(4,1)S(1)} %copy-done.325, f32[6,512,512]{1,2,0:T(8,128)} %copy-done.9, f32[6,512]{1,0:T(8,128)S(1)} %copy-done.350, bf16[512,6,64]{0,2,1:T(8,128)(2,1)S(1)} %bitcast.1079, bf16[512,6,64]{0,2,1:T(8,128)(2,1)} %bitcast.1090, ...), kind=kOutput, calls=%fused_computation.8 | convolution fusion | flops 423104000 | bytes 10760240 | tf_op jit(solution)/shard_map/sub | solution.py:114
  540.9 41.4 %psum.108 = f32[6,64]{1,0:T(8,128)S(1)} all-reduce(f32[6,64]{1,0:T(8,128)S(1)} %bitcast.1114), channel_id=1, replica_groups=mesh['section'=2,'dp'=16] {'dp'}, use_global_device_ids=true, to_apply=%region_56.57 | all-reduce | flops 384 | bytes 3072 | tf_op jit(solution)/shard_map/psum | solution.py:337
  582.7 3.4 fusion.407
  586.7 38.8 %all-reduce = (f32[6,64]{1,0:T(8,128)S(1)}, f32[1,384]{1,0:T(1,128)}, f32[1,6,2]{1,2,0:T(2,128)}, f32[1,384]{1,0:T(1,128)}) all-reduce(f32[6,64]{1,0:T(8,128)S(1)} %bitcast.1111, f32[1,384]{1,0:T(1,128)S(1)} %broadcast_in_dim.617, f32[1,6,2]{1,2,0:T(2,128)S(1)} %fusion.382, ...), channel_id=1, replica_groups=mesh['section'=2,'dp'=16] {'dp'}, use_global_device_ids=true, to_apply=%region_58.59 | all-reduce | flops 1164 | bytes 9312 | tf_op jit(solution)/shard_map/psum | solution.py:342
  625.9 6.8 select_bitcast_fusion
  632.7 6.1 copy.233
  638.8 122.0 %all-reduce.5.cloned.1.call-done = (f32[1,384,384]{2,1,0:T(8,128)}, f32[1,384,384]{2,1,0:T(8,128)}, f32[1,384,384]{2,1,0:T(8,128)}, f32[1,384,384]{2,1,0:T(8,128...) async-done(((f32[1,384,384]{2,1,0:T(8,128)}, f32[1,384,384]{2,1,0:T(8,128)}, f32[1,384,384]{2,1,0:T(8,128)}, f32[1,384,384]{2,1,0:T(8,128)}, ...) | async-done | bytes 7077904 | tf_op jit(solution)/shard_map/psum | solution.py:444
  (1245 shorter events, 350.5 us)
Async XLA Ops:
  7.2 120.8 %copy-start = (bf16[1,1024,384]{2,1,0:T(8,128)(2,1)S(1)}, bf16[1,1024,384]{2,1,0:T(8,128)(2,1)}, u32[]{:S(2)}) copy-start(bf16[1,1024,384]{2,1,0:T(8,128)(2,1)} %param.29) | copy-start | bytes 2359300
  7.2 753.6 %all-reduce.5.cloned.1.call-start = ((), (), s32[]{:S(2)}) async-start(), calls=%async_computation | async-start | bytes 14155776 | tf_op jit(solution)/shard_map/psum | solution.py:444
  27.1 83.7 %copy-start.2 = (bf16[6,512,384]{1,2,0:T(8,128)(2,1)}, bf16[6,512,384]{1,2,0:T(8,128)(2,1)S(1)}, u32[]{:S(2)}) copy-start(bf16[6,512,384]{1,2,0:T(8,128)(2,1)S(1)} %copy.169) | copy-start | bytes 7077892
  71.9 38.6 %copy-start.358 = (f32[6,64]{1,0:T(8,128)}, f32[6,64]{1,0:T(8,128)S(1)}, u32[]{:S(2)}) copy-start(f32[6,64]{1,0:T(8,128)S(1)} %get-tuple-element.95) | copy-start | bytes 4612
  72.3 39.2 %copy-start.315 = (f32[6,1,512]{2,0,1:T(8,128)}, f32[6,1,512]{2,0,1:T(8,128)S(1)}, u32[]{:S(2)}) copy-start(f32[6,1,512]{2,0,1:T(8,128)S(1)} %copy.350) | copy-start | bytes 36868
  111.5 36.9 %copy-start.8 = (f32[6,512,384]{1,2,0:T(8,128)}, f32[6,512,384]{1,2,0:T(8,128)S(1)}, u32[]{:S(2)}) copy-start(f32[6,512,384]{1,2,0:T(8,128)S(1)} %fusion.16) | copy-start | bytes 14155780
  115.7 18.3 %copy-start.307 = (f32[512,32]{0,1:T(8,128)}, f32[512,32]{0,1:T(8,128)S(1)}, u32[]{:S(2)}) copy-start(f32[512,32]{0,1:T(8,128)S(1)} %get-tuple-element.236) | copy-start | bytes 196612
  115.7 34.8 %copy-start.309 = (f32[512,32]{0,1:T(8,128)}, f32[512,32]{0,1:T(8,128)S(1)}, u32[]{:S(2)}) copy-start(f32[512,32]{0,1:T(8,128)S(1)} %get-tuple-element.235) | copy-start | bytes 196612
  117.7 16.6 %copy-start.327 = (pred[512,512]{0,1:T(8,128)(4,1)}, pred[512,512]{0,1:T(8,128)(4,1)S(1)}, u32[]{:S(2)}) copy-start(pred[512,512]{0,1:T(8,128)(4,1)S(1)} %get-tuple-element.169) | copy-start | bytes 786436
  128.6 2.6 collective-permute-start
  144.8 3.6 collective-permute-start.1
  166.4 16.6 %collective-permute-start.2 = (bf16[512,384]{0,1:T(8,128)(2,1)}, bf16[512,384]{0,1:T(8,128)(2,1)}, u32[]{:S(2)}, u32[]{:S(2)}) collective-permute-start(bf16[512,384]{0,1:T(8,128)(2,1)} %get-tuple-element.337), channel_id=1, source_target_pairs={{0,16},{1,17},{2,18},{3,19},{4,20},{5,21},{6,22},{7,23},{8,24},{9,... | collective-permute-start | bytes 1179656 | tf_op jit(solution)/shard_map/ppermute | solution.py:20
  201.4 2.7 collective-permute-start.3
  219.1 3.5 collective-permute-start.4
  237.7 3.6 collective-permute-start.5
  287.3 12.1 %collective-permute-start.6 = (bf16[512,384]{0,1:T(8,128)(2,1)}, bf16[512,384]{0,1:T(8,128)(2,1)}, u32[]{:S(2)}, u32[]{:S(2)}) collective-permute-start(bf16[512,384]{0,1:T(8,128)(2,1)} %add_convert_fusion), channel_id=1, source_target_pairs={{16,0},{17,1},{18,2},{19,3},{20,4},{21,5},{22,6},{23,7},{24,8},{25... | collective-permute-start | bytes 1179656 | tf_op jit(solution)/shard_map/ppermute | solution.py:20
  335.5 4.4 collective-permute-start.7
  373.8 4.4 collective-permute-start.8
  411.2 4.4 collective-permute-start.9
  448.2 4.4 collective-permute-start.10
  486.3 4.5 collective-permute-start.11
  539.4 42.9 %copy-start.359 = (f32[6,64]{1,0:T(8,128)S(1)}, f32[6,64]{1,0:T(8,128)}, u32[]{:S(2)}) copy-start(f32[6,64]{1,0:T(8,128)} %copy-done.358) | copy-start | bytes 4612
  539.4 42.9 %copy-start.361 = (f32[6,64]{1,0:T(8,128)S(1)}, f32[6,64]{1,0:T(8,128)}, u32[]{:S(2)}) copy-start(f32[6,64]{1,0:T(8,128)} %copy-done.360) | copy-start | bytes 4612
  539.5 43.2 %copy-start.349 = (f32[6,1,512]{2,0,1:T(8,128)S(1)}, f32[6,1,512]{2,0,1:T(8,128)}, u32[]{:S(2)}) copy-start(f32[6,1,512]{2,0,1:T(8,128)} %copy-done.348) | copy-start | bytes 36868
  (416 other events, 1325.3 us)
Sparse Core Ops, SparseCore 0:
  528.6 232.0 all-reduce.4
where the time goes:
time: 785 us; the launch traced here: 778 us
  matrix products  300 us (38%)
  blocking collectives  161 us (21%)
  waiting for transfers between devices  126 us (16%)
  local copies, waits for them, and re-layouts  84.2 us (11%)
  other arithmetic  64.8 us (8%)
  starting transfers between devices  22.6 us (3%)
  between operations  20 us (3%)
    psum x1, waiting for transfers between devices, per_device(): lax.psum((feed_acc[0], feed_acc[1], feed_acc[2], feed_acc[3], attention_a...  122 us
    sub x7, matrix products, attention_backward(): softmax_grad - inner_sum  77.2 us
    unnamed x880, local copies, waits for them, and re-layouts  75.5 us
    dot_general x49, matrix products, matmul_left(): lax.dot_general(left, right, (((0,), (0,)), ((), ())), preferred_element_...  75.2 us
    psum x1, blocking collectives, standardize(): counts, series_totals = lax.psum((counts_here, totals_here), 'dp')  44 us
    psum x1, blocking collectives, standardize_backward(): lax.psum(series_sum(one_hot, jnp.sum(upstream * centred, axis=-1)), 'dp')  41.4 us
    dot_general x49, matrix products, matmul(): return jnp.dot(left, right, preferred_element_type=jnp.float32)  39.2 us
    psum x1, blocking collectives, standardize_backward(): lax.psum(series_sum(one_hot, jnp.sum(centred_grad, axis=-1)), 'dp')  38.8 us
  transfers between devices with their start and end apart: 13, of which 6 were waited for; matrix products, arithmetic and copies ran while one was open for 9% of the time, Pallas kernels for 0%

commit v1 on v0

v1 whole, which is shorter than its diff:
```python
import functools

import jax
import jax.numpy as jnp
from jax import lax
from jax.experimental import pallas as pl
from jax.experimental.pallas import tpu as pltpu
from jax.sharding import PartitionSpec as P

HD = 64
BLOCK = 512
SER_DEV = 4
LANES = 128
CHUNK = 256

norm_epsilon = 1e-05
scale_epsilon = 1e-05
masked_score = -1e30

f32 = jnp.float32
bf16 = jnp.bfloat16

AS_IS = (((1,), (0,)), ((), ()))
RIGHT_T = (((1,), (1,)), ((), ()))
LEFT_T = (((0,), (0,)), ((), ()))


def dot(left, right, dims=AS_IS):
    return lax.dot_general(left, right, dims, preferred_element_type=f32)


def column(row):
    return jnp.broadcast_to(row.astype(f32), (LANES, row.shape[1])).T


def lane_index(rows):
    return lax.broadcasted_iota(jnp.int32, (rows, LANES), 1)


def swap_halves(x):
    low_half = (lane_index(x.shape[0]) % HD) < HD // 2
    return jnp.where(low_half, pltpu.roll(x, LANES - HD // 2, 1), pltpu.roll(x, HD // 2, 1))


def turn(x, cosine, sine):
    return x * cosine + swap_halves(x) * sine


def turn_back(x, cosine, sine):
    return x * cosine - swap_halves(x) * sine


def inverse_rms(x):
    return lax.rsqrt(jnp.mean(x * x, axis=1, keepdims=True) + norm_epsilon)


def series_hits(sid_col, piece):
    return sid_col == (lane_index(sid_col.shape[0]) + piece * LANES).astype(f32)


def rows_of(hits, per_series):
    return jnp.sum(jnp.where(hits, per_series, 0.0), axis=1, keepdims=True)


def series_of(hits, per_row):
    return jnp.sum(jnp.where(hits, per_row, 0.0), axis=0, keepdims=True)


def stats_body(x_ref, sid_ref, out_ref):
    i = pl.program_id(0)
    x = x_ref[0].astype(f32)
    width = x.shape[1]
    sid_col = column(sid_ref[pl.ds(i, 1), :])
    pieces = out_ref.shape[-1] // LANES
    totals = jnp.sum(x, axis=1, keepdims=True)
    centre = jnp.zeros_like(totals)
    out_ref[0] = jnp.zeros(out_ref.shape[1:], f32)
    for piece in range(pieces):
        hits = series_hits(sid_col, piece)
        count = series_of(hits, 1.0)
        total = series_of(hits, totals)
        centre = centre + rows_of(hits, total / (jnp.maximum(count, 1.0) * width))
        out_ref[0, 0:1, piece * LANES : (piece + 1) * LANES] = count
        out_ref[0, 1:2, piece * LANES : (piece + 1) * LANES] = total
    centred = x - centre
    squares = jnp.sum(centred * centred, axis=1, keepdims=True)
    for piece in range(pieces):
        hits = series_hits(sid_col, piece)
        out_ref[0, 2:3, piece * LANES : (piece + 1) * LANES] = series_of(hits, squares)


def merge_stats(here, there, width):
    count_a, total_a, spread_a = here[:, 0], here[:, 1], here[:, 2]
    count_b, total_b, spread_b = there[:, 0], there[:, 1], there[:, 2]
    count = count_a + count_b
    gap = total_a / (jnp.maximum(count_a, 1.0) * width) - total_b / (
        jnp.maximum(count_b, 1.0) * width
    )
    weight = count_a * count_b * width / jnp.maximum(count, 1.0)
    spread = spread_a + spread_b + gap * gap * weight
    rest = jnp.zeros_like(here[:, 3:])
    return jnp.concatenate(
        [jnp.stack([count, total_a + total_b, spread], axis=1), rest], axis=1
    )


def centre_and_scale(stats, width):
    entries = jnp.maximum(stats[0:1], 1.0) * width
    centre = stats[1:2] / entries
    scaling = jnp.sqrt(stats[2:3] / entries + scale_epsilon)
    return entries, centre, scaling


def load_weights(take_own, own_refs, other_refs, scratch_refs, sems):
    @pl.when(pl.program_id(0) == 0)
    def _():
        @pl.when(take_own)
        def _():
            for k, (src, dst) in enumerate(zip(own_refs, scratch_refs)):
                pltpu.make_async_copy(src, dst, sems.at[k]).start()

        @pl.when(jnp.logical_not(take_own))
        def _():
            for k, (src, dst) in enumerate(zip(other_refs, scratch_refs)):
                pltpu.make_async_copy(src, dst, sems.at[k]).start()

        for k, (src, dst) in enumerate(zip(own_refs, scratch_refs)):
            pltpu.make_async_copy(src, dst, sems.at[k]).wait()


def fill_same(var_row, same_ref):
    rows = same_ref.shape[0]
    var_col = column(var_row)
    row = var_row.astype(f32)
    for piece in range(rows // LANES):
        part = row[:, piece * LANES : (piece + 1) * LANES]
        same_ref[:, piece * LANES : (piece + 1) * LANES] = jnp.where(var_col == part, 1.0, 0.0)


def attention_forward(
    hidden, gains, cosine, sine, item_row, var_row, bias_ref, big_ref, same_ref, sums_ref,
    qkv_ref, prob_ref, inv_ref, mixed_ref,
):
    rows, width = hidden.shape
    pairs = width // LANES
    normed = (hidden * inverse_rms(hidden) * gains).astype(bf16)
    qkv = dot(normed, big_ref[:, : 3 * width])
    for p in range(pairs):
        at = p * LANES
        q = turn(qkv[:, at : at + LANES], cosine, sine)
        k = turn(qkv[:, width + at : width + at + LANES], cosine, sine)
        qkv_ref[0, :, at : at + LANES] = (q * HD**-0.5).astype(bf16)
        qkv_ref[0, :, width + at : width + at + LANES] = k.astype(bf16)
        qkv_ref[0, :, 2 * width + at : 2 * width + at + LANES] = qkv[
            :, 2 * width + at : 2 * width + at + LANES
        ].astype(bf16)
    fill_same(var_row, same_ref)
    lane = lane_index(rows)
    second = jnp.where(column(item_row) > 0.0, 1.0, 0.0)
    item_q = jnp.where(lane == 0, second, jnp.where(lane == 1, 1.0 - second, 0.0)).astype(bf16)
    item_k = jnp.where(
        lane == 0, (1.0 - second) * masked_score, jnp.where(lane == 1, second * masked_score, 0.0)
    ).astype(bf16)
    extra = lax.broadcasted_iota(jnp.int32, (16, rows), 0)
    sums_ref[...] = jnp.ones_like(sums_ref)
    for p in range(pairs):
        at = p * LANES
        q_pair = qkv_ref[0, :, at : at + LANES]
        k_pair = jnp.concatenate([qkv_ref[0, :, width + at : width + at + LANES], item_k], axis=1)
        v_turned = qkv_ref[0, :, 2 * width + at : 2 * width + at + LANES].T
        first_rows = lax.broadcasted_iota(jnp.int32, (LANES, rows), 0) < HD
        attended = None
        for half in range(2):
            head = 2 * p + half
            mine = (lane // HD) == half
            q_aug = jnp.concatenate([jnp.where(mine, q_pair, 0.0).astype(bf16), item_q], axis=1)
            scores = dot(k_pair, q_aug, RIGHT_T)
            scores = scores + same_ref[...] * (bias_ref[2 * head] - bias_ref[2 * head + 1])
            peak = jnp.max(scores, axis=0, keepdims=True)
            prob = jnp.exp(scores - peak).astype(bf16)
            prob_ref[0, head] = prob
            own_rows = first_rows if half == 0 else jnp.logical_not(first_rows)
            v_aug = jnp.concatenate(
                [
                    jnp.where(own_rows, v_turned, 0.0).astype(bf16),
                    jnp.where(extra == half, 1.0, 0.0).astype(bf16),
                ],
                axis=0,
            )
            part = dot(v_aug, prob)
            attended = part if attended is None else attended + part
        inv_a = 1.0 / attended[LANES : LANES + 1]
        inv_b = 1.0 / attended[LANES + 1 : LANES + 2]
        sums_ref[2 * p : 2 * p + 1, :] = inv_a
        sums_ref[2 * p + 1 : 2 * p + 2, :] = inv_b
        mixed_t = attended[:LANES] * jnp.where(first_rows, inv_a, inv_b)
        mixed_ref[0, :, at : at + LANES] = mixed_t.T.astype(bf16)
    inv_ref[0] = sums_ref[...].T
    return hidden + dot(mixed_ref[0], big_ref[:, 3 * width : 4 * width])


def sigmoid(x):
    return 0.5 * jnp.tanh(0.5 * x) + 0.5


def feed_forward(middle, gains, big_ref, down_ref):
    width = middle.shape[1]
    hidden = down_ref.shape[0]
    feed = (middle * inverse_rms(middle) * gains).astype(bf16)
    total = middle
    for at in range(0, hidden, CHUNK):
        gate = dot(feed, big_ref[:, 4 * width + at : 4 * width + at + CHUNK])
        up = dot(feed, big_ref[:, 4 * width + hidden + at : 4 * width + hidden + at + CHUNK])
        active = (gate * sigmoid(gate) * up).astype(bf16)
        total = total + dot(active, down_ref[at : at + CHUNK, :])
    return total.astype(bf16)


def feed_both(middle, gains, grad_low, big_ref, down_ref, gate_acc, up_acc, down_acc, gain_acc, with_result):
    width = middle.shape[1]
    hidden = down_ref.shape[0]
    inverse = inverse_rms(middle)
    feed = (middle * inverse * gains).astype(bf16)
    feed_t = feed.T
    total = middle
    feed_grad = jnp.zeros(middle.shape, f32)
    for at in range(0, hidden, CHUNK):
        gate_w = big_ref[:, 4 * width + at : 4 * width + at + CHUNK]
        up_w = big_ref[:, 4 * width + hidden + at : 4 * width + hidden + at + CHUNK]
        down_w = down_ref[at : at + CHUNK, :]
        gate = dot(feed, gate_w)
        up = dot(feed, up_w)
        act_grad = dot(grad_low, down_w, RIGHT_T)
        gated = sigmoid(gate)
        swish = gate * gated
        active = (swish * up).astype(bf16)
        gate_grad = (act_grad * up * (gated + swish * (1.0 - gated))).astype(bf16)
        up_grad = (act_grad * swish).astype(bf16)
        if with_result:
            total = total + dot(active, down_w)
        feed_grad = feed_grad + dot(gate_grad, gate_w, RIGHT_T) + dot(up_grad, up_w, RIGHT_T)
        gate_acc[:, at : at + CHUNK] += dot(feed_t, gate_grad)
        up_acc[:, at : at + CHUNK] += dot(feed_t, up_grad)
        down_acc[at : at + CHUNK, :] += dot(active, grad_low, LEFT_T)
    scaled = feed_grad * gains
    gain_acc[...] += jnp.sum(feed_grad * middle * inverse, axis=0, keepdims=True)
    middle_grad = (
        grad_low.astype(f32)
        + inverse * scaled
        - middle * (inverse * inverse * inverse) * jnp.mean(scaled * middle, axis=1, keepdims=True)
    )
    return total, middle_grad


def attention_backward(
    middle_grad, hidden, gains, cosine, sine, var_row, big_ref, same_ref,
    qkv_ref, prob_ref, inv_ref, mixed_ref, grads_ref, qkv_acc, out_acc, gain_acc, bias_acc,
):
    rows, width = hidden.shape
    pairs = width // LANES
    inverse = inverse_rms(hidden)
    normed = (hidden * inverse * gains).astype(bf16)
    mix_grad = middle_grad.astype(bf16)
    out_acc[...] += dot(mixed_ref[0], mix_grad, LEFT_T)
    att_grad = dot(mix_grad, big_ref[:, 3 * width : 4 * width], RIGHT_T).astype(bf16)
    fill_same(var_row, same_ref)
    lane = lane_index(rows)
    ones_two = jnp.where(lane < 2, 1.0, 0.0).astype(bf16)
    first_rows = lax.broadcasted_iota(jnp.int32, (LANES, rows), 0) < HD
    for p in range(pairs):
        at = p * LANES
        q_pair = qkv_ref[0, :, at : at + LANES]
        k_turned = qkv_ref[0, :, width + at : width + at + LANES].T
        v_aug = jnp.concatenate(
            [qkv_ref[0, :, 2 * width + at : 2 * width + at + LANES], ones_two], axis=1
        )
        grad_pair = att_grad[:, at : at + LANES].astype(f32)
        product = grad_pair * mixed_ref[0, :, at : at + LANES].astype(f32)
        value_grad = key_grad = query_grad_t = None
        for half in range(2):
            head = 2 * p + half
            mine = (lane // HD) == half
            inv = inv_ref[0, :, head : head + 1]
            inner = jnp.sum(jnp.where(mine, product, 0.0), axis=1, keepdims=True) * inv
            grad_low = jnp.where(mine, grad_pair * inv, 0.0).astype(bf16)
            inner_high = inner.astype(bf16).astype(f32)
            tail = jnp.where(
                lane == 0, -inner_high, jnp.where(lane == 1, inner_high - inner, 0.0)
            ).astype(bf16)
            prob = prob_ref[0, head]
            prob_grad = dot(v_aug, jnp.concatenate([grad_low, tail], axis=1), RIGHT_T)
            score_grad = prob.astype(f32) * prob_grad
            bias_acc[head : head + 1, :] += jnp.sum(
                score_grad * same_ref[...], axis=0, keepdims=True
            )
            score_low = score_grad.astype(bf16)
            own_rows = first_rows if half == 0 else jnp.logical_not(first_rows)
            q_mine = jnp.where(mine, q_pair, 0.0).astype(bf16)
            k_mine = jnp.where(own_rows, k_turned, 0.0).astype(bf16)
            part_v = dot(prob, grad_low)
            part_k = dot(score_low, q_mine)
            part_q = dot(k_mine, score_low)
            value_grad = part_v if value_grad is None else value_grad + part_v
            key_grad = part_k if key_grad is None else key_grad + part_k
            query_grad_t = part_q if query_grad_t is None else query_grad_t + part_q
        query_grad = query_grad_t.T * HD**-0.5
        grads_ref[:, at : at + LANES] = turn_back(query_grad, cosine, sine).astype(bf16)
        grads_ref[:, width + at : width + at + LANES] = turn_back(key_grad, cosine, sine).astype(
            bf16
        )
        grads_ref[:, 2 * width + at : 2 * width + at + LANES] = value_grad.astype(bf16)
    qkv_acc[...] += dot(normed, grads_ref[...], LEFT_T)
    normed_grad = dot(grads_ref[...], big_ref[:, : 3 * width], RIGHT_T)
    scaled = normed_grad * gains
    gain_acc[...] += jnp.sum(normed_grad * hidden * inverse, axis=0, keepdims=True)
    return (
        middle_grad
        + inverse * scaled
        - hidden * (inverse * inverse * inverse) * jnp.mean(scaled * hidden, axis=1, keepdims=True)
    )


def pack(sec, out_ref, tiles):
    half = out_ref.shape[1]
    at = 0
    for tile in tiles:
        rows = tile.shape[0]
        slot = sec if at < half else 1 - sec
        start = at % half
        out_ref[slot, start : start + rows, :] = tile.astype(bf16)
        at += rows


def column_tiles(acc_ref, first=0, width=None):
    width = acc_ref.shape[1] if width is None else width
    return [acc_ref[:, first + at : first + at + LANES] for at in range(0, width, LANES)]


def first_layer_body(
    sec_ref, bias_ref, x_ref, sid_ref, item_ref, var_ref, stats_ref, cos_ref, sin_ref, gain_ref,
    own_big, other_big, own_down, other_down,
    result_ref, hidden_ref, qkv_ref, prob_ref, inv_ref, mixed_ref, middle_ref,
    big_ref, down_ref, same_ref, sums_ref, sems,
):
    i = pl.program_id(0)
    m = 3 * sec_ref[0] + i
    load_weights(
        sec_ref[0] == 0, (own_big, own_down), (other_big, other_down), (big_ref, down_ref), sems
    )
    x = x_ref[0].astype(f32)
    width = x.shape[1]
    _, centre, scaling = centre_and_scale(stats_ref[0], width)
    sid_col = column(sid_ref[pl.ds(m, 1), :])
    centre_rows = scale_rows = 0.0
    for piece in range(stats_ref.shape[-1] // LANES):
        hits = series_hits(sid_col, piece)
        part = slice(piece * LANES, (piece + 1) * LANES)
        centre_rows = centre_rows + rows_of(hits, centre[:, part])
        scale_rows = scale_rows + rows_of(hits, scaling[:, part])
    hidden = (x - centre_rows) / scale_rows
    hidden_ref[0] = hidden
    middle = attention_forward(
        hidden, gain_ref[0:1, :], cos_ref[0], sin_ref[0],
        item_ref[pl.ds(m, 1), :], var_ref[pl.ds(m, 1), :], bias_ref, big_ref, same_ref, sums_ref,
        qkv_ref, prob_ref, inv_ref, mixed_ref,
    )
    middle_ref[0] = middle
    result_ref[0] = feed_forward(middle, gain_ref[1:2, :], big_ref, down_ref)


def second_layer_body(
    sec_ref, bias_ref, h_ref, grad_ref, item_ref, var_ref, cos_ref, sin_ref, gain_ref,
    own_big, other_big, own_down, other_down,
    result_ref, qkv_ref, prob_ref, inv_ref, mixed_ref, middle_grad_ref, pack_ref, small_ref,
    big_ref, down_ref, same_ref, sums_ref, gate_acc, up_acc, down_acc, gain_acc, sems,
):
    i = pl.program_id(0)
    m = 3 * sec_ref[0] + i
    load_weights(
        sec_ref[0] == 1, (own_big, own_down), (other_big, other_down), (big_ref, down_ref), sems
    )

    @pl.when(i == 0)
    def _():
        for acc in (gate_acc, up_acc, down_acc, gain_acc):
            acc[...] = jnp.zeros_like(acc)

    middle = attention_forward(
        h_ref[0].astype(f32), gain_ref[0:1, :], cos_ref[0], sin_ref[0],
        item_ref[pl.ds(m, 1), :], var_ref[pl.ds(m, 1), :], bias_ref, big_ref, same_ref, sums_ref,
        qkv_ref, prob_ref, inv_ref, mixed_ref,
    )
    total, middle_grad = feed_both(
        middle, gain_ref[1:2, :], grad_ref[0], big_ref, down_ref,
        gate_acc, up_acc, down_acc, gain_acc, True,
    )
    result_ref[0] = total.astype(bf16)
    middle_grad_ref[0] = middle_grad
    finish_feed(i, sec_ref[0], pack_ref, small_ref, gate_acc, up_acc, down_acc, gain_acc)


def finish_feed(i, sec, pack_ref, small_ref, gate_acc, up_acc, down_acc, gain_acc):
    @pl.when(i == pl.num_programs(0) - 1)
    def _():
        pack(
            sec, pack_ref,
            column_tiles(gate_acc) + column_tiles(up_acc) + column_tiles(down_acc),
        )
        small_ref[...] = jnp.broadcast_to(gain_acc[...], small_ref.shape)


def feed_backward_body(
    sec_ref, middle_ref, grad_ref, gain_ref, own_big, other_big, own_down, other_down,
    middle_grad_ref, pack_ref, small_ref,
    big_ref, down_ref, gate_acc, up_acc, down_acc, gain_acc, sems,
):
    i = pl.program_id(0)
    load_weights(
        sec_ref[0] == 0, (own_big, own_down), (other_big, other_down), (big_ref, down_ref), sems
    )

    @pl.when(i == 0)
    def _():
        for acc in (gate_acc, up_acc, down_acc, gain_acc):
            acc[...] = jnp.zeros_like(acc)

    _, middle_grad = feed_both(
        middle_ref[0], gain_ref[1:2, :], grad_ref[0], big_ref, down_ref,
        gate_acc, up_acc, down_acc, gain_acc, False,
    )
    middle_grad_ref[0] = middle_grad
    finish_feed(i, sec_ref[0], pack_ref, small_ref, gate_acc, up_acc, down_acc, gain_acc)


def attention_backward_body(
    layer, sec_ref, middle_grad_ref, h_ref, qkv_ref, prob_ref, inv_ref, mixed_ref, sid_ref, var_ref,
    cos_ref, sin_ref, gain_ref, own_big, other_big,
    grad_ref, series_ref, pack_ref, small_ref,
    big_ref, same_ref, grads_ref, qkv_acc, out_acc, gain_acc, bias_acc, sems,
):
    i = pl.program_id(0)
    m = 3 * sec_ref[0] + i
    width = h_ref.shape[2]
    attention_part = pl.ds(0, 4 * width)
    load_weights(
        sec_ref[0] == layer, (own_big.at[:, attention_part],), (other_big.at[:, attention_part],),
        (big_ref,), sems,
    )

    @pl.when(i == 0)
    def _():
        for acc in (qkv_acc, out_acc, gain_acc, bias_acc):
            acc[...] = jnp.zeros_like(acc)

    hidden = h_ref[0].astype(f32)
    hidden_grad = attention_backward(
        middle_grad_ref[0], hidden, gain_ref[0:1, :], cos_ref[0], sin_ref[0],
        var_ref[pl.ds(m, 1), :], big_ref, same_ref,
        qkv_ref, prob_ref, inv_ref, mixed_ref, grads_ref, qkv_acc, out_acc, gain_acc, bias_acc,
    )
    grad_ref[0] = hidden_grad.astype(grad_ref.dtype)
    if layer == 0:
        sid_col = column(sid_ref[pl.ds(m, 1), :])
        grad_rows = jnp.sum(hidden_grad, axis=1, keepdims=True)
        cross_rows = jnp.sum(hidden_grad * hidden, axis=1, keepdims=True)
        hidden_rows = jnp.sum(hidden, axis=1, keepdims=True)
        series_ref[0] = jnp.zeros(series_ref.shape[1:], f32)
        for piece in range(series_ref.shape[-1] // LANES):
            hits = series_hits(sid_col, piece)
            part = slice(piece * LANES, (piece + 1) * LANES)
            series_ref[0, 0:1, part] = series_of(hits, grad_rows)
            series_ref[0, 1:2, part] = series_of(hits, cross_rows)
            series_ref[0, 2:3, part] = series_of(hits, hidden_rows)
    else:
        series_ref[0] = jnp.zeros(series_ref.shape[1:], f32)

    @pl.when(i == pl.num_programs(0) - 1)
    def _():
        tiles = []
        for first in range(0, 3 * width, width):
            tiles += column_tiles(qkv_acc, first, width)
        pack(sec_ref[0], pack_ref, tiles + column_tiles(out_acc))
        small_ref[...] = jnp.zeros_like(small_ref)
        small_ref[0:1, :] = gain_acc[...]
        bias_sums = jnp.sum(bias_acc[...], axis=1, keepdims=True)
        small_ref[8:16, :] = jnp.broadcast_to(bias_sums, (8, width))


def final_body(
    sec_ref, x_ref, sid_ref, stats_ref, series_ref, own_first, own_second, other_grad,
    own_out, other_out, out_ref, grads_ref,
):
    i = pl.program_id(0)
    sec = sec_ref[0]
    own = (i // 3) == sec
    grads_ref[0] = jnp.where(own, own_out[0], other_out[0])
    grad = jnp.where(
        own,
        jnp.where(sec == 0, own_first[0], own_second[0].astype(f32)),
        other_grad[0].astype(f32),
    )

    @pl.when(sec == 0)
    def _():
        x = x_ref[0].astype(f32)
        width = x.shape[1]
        entries, centre, scaling = centre_and_scale(stats_ref[0], width)
        sums = series_ref[0]
        cross = sums[1:2] * scaling
        spread_grad = -cross / (2.0 * scaling * scaling * scaling * entries)
        mean_grad = sums[0:1] / scaling + 2.0 * spread_grad * (sums[2:3] * scaling)
        tables = (centre, 1.0 / scaling, 2.0 * spread_grad, mean_grad / entries)
        sid_col = column(sid_ref[pl.ds(i, 1), :])
        looked = [0.0, 0.0, 0.0, 0.0]
        for piece in range(stats_ref.shape[-1] // LANES):
            hits = series_hits(sid_col, piece)
            part = slice(piece * LANES, (piece + 1) * LANES)
            for k in range(4):
                looked[k] = looked[k] + rows_of(hits, tables[k][:, part])
        out_ref[0] = grad * looked[1] + (x - looked[0]) * looked[2] - looked[3]

    @pl.when(sec != 0)
    def _():
        out_ref[0] = grad


def unpack_body(low_ref, high_ref, *out_refs):
    half = low_ref.shape[0]
    at = 0
    for out_ref in out_refs:
        rows, width = out_ref.shape
        for col in range(0, width, LANES):
            source = low_ref if at < half else high_ref
            start = at % half
            out_ref[:, col : col + LANES] = source[start : start + rows, :].astype(f32)
            at += rows


def swapped(x):
    return lax.ppermute(x, "section", [(0, 1), (1, 0)])


def exchange_steps(count):
    bits = []
    step = 1
    while step < count:
        bits.append(step)
        step *= 2
    first = list(bits)
    second = list(bits)
    for k in range(0, len(bits) - 1, 2):
        second[k], second[k + 1] = bits[k + 1], bits[k]
    return first, second


def partner(x, by_first, by_second, count):
    pairs = [(i, i ^ by_first) for i in range(count)]
    pairs += [(count + i, count + (i ^ by_second)) for i in range(count)]
    return lax.ppermute(x, ("section", "dp"), pairs)


def sum_over_dp(kept, sec, index, count):
    first, second = exchange_steps(count)
    current = kept
    for a, b in zip(first, second):
        step = jnp.where(sec == 0, a, b)
        bit = (index // step) % 2
        half = current.shape[0] // 2
        keep = lax.dynamic_slice_in_dim(current, bit * half, half, 0)
        send = lax.dynamic_slice_in_dim(current, (1 - bit) * half, half, 0)
        got = partner(send, a, b, count)
        current = (keep.astype(f32) + got.astype(f32)).astype(bf16)
    for a, b in zip(reversed(first), reversed(second)):
        step = jnp.where(sec == 0, a, b)
        bit = (index // step) % 2
        got = partner(current, a, b, count)
        low = jnp.where(bit == 0, current, got)
        high = jnp.where(bit == 0, got, current)
        current = jnp.concatenate([low, high], axis=0)
    return current


def sum_halves(packed, sec, index, count):
    kept = (packed[0].astype(f32) + swapped(packed[1]).astype(f32)).astype(bf16)
    return sum_over_dp(kept, sec, index, count)


HBM = pl.BlockSpec(memory_space=pl.ANY)
SCALARS = pl.BlockSpec(memory_space=pltpu.SMEM)


def whole_block(shape):
    return pl.BlockSpec(shape, lambda i, *_: (0,) * len(shape))


def by_step(shape):
    return pl.BlockSpec((1,) + shape, lambda i, *_: (i,) + (0,) * len(shape))


def by_batch(shape):
    return pl.BlockSpec((1,) + shape, lambda i, s: (3 * s[0] + i,) + (0,) * len(shape))


def call(body, grid, in_specs, out_specs, out_shapes, scratch, flops, name):
    return pl.pallas_call(
        body,
        grid_spec=pltpu.PrefetchScalarGridSpec(
            num_scalar_prefetch=1,
            grid=(grid,),
            in_specs=in_specs,
            out_specs=out_specs,
            scratch_shapes=scratch,
        ),
        out_shape=out_shapes,
        compiler_params=pltpu.CompilerParams(vmem_limit_bytes=58 * 2**20),
        cost_estimate=pl.CostEstimate(flops=flops, bytes_accessed=2**22, transcendentals=0),
        name=name,
    )


def per_device(
    inputs,
    series_id,
    item_offset,
    variate_offset,
    cotangent,
    attention_gain,
    query_weight,
    key_weight,
    value_weight,
    out_weight,
    variate_bias,
    feed_gain,
    gate_weight,
    up_weight,
    down_weight,
):
    sec = lax.axis_index("section")
    index = lax.axis_index("dp")
    count = lax.axis_size("dp")
    on_first = sec == 0
    sec_arr = sec.astype(jnp.int32).reshape(1)
    micro, rows, width = inputs.shape
    own_micro = micro // 2
    heads = variate_bias.shape[1]
    hidden = down_weight.shape[1]
    series_count = SER_DEV * count
    lanes_series = -(-series_count // LANES) * LANES
    stats_shape = (8, lanes_series)
    all_rows = whole_block((micro, rows))

    own_big = jnp.concatenate(
        [w[0] for w in (query_weight, key_weight, value_weight, out_weight, gate_weight, up_weight)],
        axis=1,
    )
    own_down = down_weight[0]
    own_small = jnp.concatenate(
        [
            attention_gain,
            feed_gain,
            jnp.pad(variate_bias.reshape(1, 2 * heads), ((0, 0), (0, width - 2 * heads))),
        ],
        axis=0,
    ).astype(f32)
    own_small = jnp.pad(own_small, ((0, 5), (0, 0)))

    stats = pl.pallas_call(
        stats_body,
        grid=(micro,),
        in_specs=[by_step((rows, width)), all_rows],
        out_specs=by_step(stats_shape),
        out_shape=jax.ShapeDtypeStruct((micro,) + stats_shape, f32),
        name="series_stats",
    )(inputs, series_id)
    for step in exchange_steps(count)[0]:
        stats = merge_stats(stats, partner(stats, step, step, count), width)

    other_small = swapped(own_small)
    other_big = swapped(own_big)
    other_down = swapped(own_down)
    small = (
        jnp.where(on_first, own_small, other_small),
        jnp.where(on_first, other_small, own_small),
    )
    bias = tuple(s[2, : 2 * heads] for s in small)
    weights = (own_big, other_big, own_down, other_down)

    own_variates = lax.dynamic_slice_in_dim(variate_offset, own_micro * sec, own_micro, 0)
    time = (jnp.arange(rows, dtype=jnp.int32) % BLOCK)[None, :] - own_variates
    lane = jnp.arange(LANES, dtype=jnp.int32)
    frequency = 10000.0 ** (-(lane % (HD // 2)).astype(f32) * (2.0 / HD))
    angle = time.astype(f32)[:, :, None] * frequency
    cosine = jnp.cos(angle)
    sine = jnp.sin(angle) * jnp.where(lane % HD < HD // 2, -1.0, 1.0)

    row_block = by_step((rows, width))
    head_block = by_step((heads, rows, rows))
    qkv_block = by_step((rows, 3 * width))
    lane_block = by_step((rows, LANES))
    weight_specs = [HBM] * 4
    gain_spec = whole_block((8, width))
    big_scratch = pltpu.VMEM(own_big.shape, bf16)
    down_scratch = pltpu.VMEM(own_down.shape, bf16)
    same_scratch = pltpu.VMEM((rows, rows), f32)
    sums_scratch = pltpu.VMEM((LANES, rows), f32)
    feed_accs = [
        pltpu.VMEM((width, hidden), f32),
        pltpu.VMEM((width, hidden), f32),
        pltpu.VMEM((hidden, width), f32),
        pltpu.VMEM((1, width), f32),
    ]
    sems = pltpu.SemaphoreType.DMA((2,))
    layer_flops = 2 * rows * (4 * width * width + 3 * width * hidden) * own_micro

    def shape(*dims, dtype=f32):
        return jax.ShapeDtypeStruct(dims, dtype)

    saved_shapes = [
        shape(own_micro, rows, 3 * width, dtype=bf16),
        shape(own_micro, heads, rows, rows, dtype=bf16),
        shape(own_micro, rows, LANES),
        shape(own_micro, rows, width, dtype=bf16),
    ]
    saved_blocks = [qkv_block, head_block, lane_block, row_block]
    row_shape = shape(own_micro, rows, width)
    low_shape = shape(own_micro, rows, width, dtype=bf16)
    feed_rows = 3 * width * hidden // LANES
    attention_rows = 4 * width * width // LANES
    feed_pack = (2, feed_rows // 2, LANES)
    attention_pack = (2, attention_rows // 2, LANES)

    result_one, standard, qkv_one, prob_one, inv_one, mixed_one, middle_one = call(
        first_layer_body, own_micro,
        [SCALARS, by_batch((rows, width)), all_rows, all_rows, all_rows, by_batch(stats_shape),
         lane_block, lane_block, gain_spec] + weight_specs,
        [row_block, row_block] + saved_blocks + [row_block],
        [low_shape, row_shape] + saved_shapes + [row_shape],
        [big_scratch, down_scratch, same_scratch, sums_scratch, sems],
        2 * layer_flops, "first_layer",
    )(sec_arr, bias[0], inputs, series_id, item_offset, variate_offset, stats, cosine, sine,
      small[0], *weights)

    result_two, qkv_two, prob_two, inv_two, mixed_two, middle_grad_two, feed_two, gain_two = call(
        second_layer_body, own_micro,
        [SCALARS, row_block, by_batch((rows, width)), all_rows, all_rows, lane_block, lane_block,
         gain_spec] + weight_specs,
        [row_block] + saved_blocks + [row_block, whole_block(feed_pack), whole_block((8, width))],
        [low_shape] + saved_shapes
        + [row_shape, shape(*feed_pack, dtype=bf16), shape(8, width)],
        [big_scratch, down_scratch, same_scratch, sums_scratch] + feed_accs + [sems],
        4 * layer_flops, "second_layer",
    )(sec_arr, bias[1], result_one, cotangent, item_offset, variate_offset, cosine, sine,
      small[1], *weights)

    def attention_back(layer, middle_grad, h, saved, dtype):
        return call(
            functools.partial(attention_backward_body, layer), own_micro,
            [row_block, row_block] + saved_blocks
            + [all_rows, all_rows, lane_block, lane_block, gain_spec, HBM, HBM],
            [row_block, by_step(stats_shape), whole_block(attention_pack), whole_block((16, width))],
            [shape(own_micro, rows, width, dtype=dtype), shape(own_micro, *stats_shape),
             shape(*attention_pack, dtype=bf16), shape(16, width)],
            [pltpu.VMEM((width, 4 * width), bf16), same_scratch,
             pltpu.VMEM((rows, 3 * width), bf16), pltpu.VMEM((width, 3 * width), f32),
             pltpu.VMEM((width, width), f32), pltpu.VMEM((1, width), f32),
             pltpu.VMEM((8, rows), f32), sems],
            2 * layer_flops, "attention_back_%d" % layer,
        )(sec_arr, middle_grad, h, *saved, series_id, variate_offset, cosine, sine, small[layer],
          own_big, other_big)

    grad_one, _, attention_two, small_two = attention_back(
        1, middle_grad_two, result_one, (qkv_two, prob_two, inv_two, mixed_two), bf16
    )

    middle_grad_one, feed_one, gain_one = call(
        feed_backward_body, own_micro,
        [row_block, row_block, gain_spec] + weight_specs,
        [row_block, whole_block(feed_pack), whole_block((8, width))],
        [row_shape, shape(*feed_pack, dtype=bf16), shape(8, width)],
        [big_scratch, down_scratch] + feed_accs + [sems],
        2 * layer_flops, "feed_back",
    )(sec_arr, middle_one, grad_one, small[0], *weights)

    standard_grad, series_sums, attention_one, small_one = attention_back(
        0, middle_grad_one, standard, (qkv_one, prob_one, inv_one, mixed_one), f32
    )

    feed_two_sum = sum_halves(feed_two, sec, index, count)
    attention_two_sum = sum_halves(attention_two, sec, index, count)
    feed_one_sum = sum_halves(feed_one, sec, index, count)
    attention_one_sum = sum_halves(attention_one, sec, index, count)

    zeros = jnp.zeros_like(series_sums)
    series_all = jnp.concatenate(
        [jnp.where(on_first, series_sums, zeros), jnp.where(on_first, zeros, series_sums)], axis=0
    )
    small_all = jnp.concatenate(
        [series_all.reshape(-1, LANES)]
        + [
            part.reshape(-1, LANES)
            for part in (small_one, gain_one, small_two, gain_two)
        ],
        axis=0,
    )
    for step in exchange_steps(count)[0]:
        small_all = small_all + partner(small_all, step, step, count)
    small_all = small_all + swapped(small_all)
    series_rows = micro * stats_shape[0] * lanes_series // LANES
    series_all = small_all[:series_rows].reshape((micro,) + stats_shape)
    rest = small_all[series_rows:].reshape(2, 24, width)
    mine = jnp.where(on_first, rest[0], rest[1])
    grad_attention_gain = mine[0:1]
    grad_feed_gain = mine[16:17]
    same_sum = mine[8 : 8 + heads, 0]
    grad_bias = jnp.stack([same_sum, -same_sum], axis=-1)[None]

    own_out = jnp.where(on_first, result_one, result_two)
    other_out = swapped(jnp.where(on_first, result_two, result_one))
    other_grad = swapped(jnp.where(on_first, grad_one, standard_grad.astype(bf16)))

    def own_step(i, s):
        return (jnp.clip(i - own_micro * s[0], 0, own_micro - 1), 0, 0)

    def other_step(i, s):
        return (jnp.clip(i - own_micro * (1 - s[0]), 0, own_micro - 1), 0, 0)

    own_spec = pl.BlockSpec((1, rows, width), own_step)
    other_spec = pl.BlockSpec((1, rows, width), other_step)
    input_grads, section_output = call(
        final_body, micro,
        [row_block, all_rows, by_step(stats_shape), by_step(stats_shape), own_spec, own_spec,
         other_spec, own_spec, other_spec],
        [row_block, row_block],
        [shape(micro, rows, width), shape(micro, rows, width, dtype=bf16)],
        [], 10**8, "final",
    )(sec_arr, inputs, series_id, stats, series_all, standard_grad, grad_one, other_grad,
      own_out, other_out)

    def whole(one, two):
        other = swapped(jnp.where(on_first, two, one))
        own = jnp.where(on_first, one, two)
        return jnp.where(on_first, own, other), jnp.where(on_first, other, own)

    def unpack(halves, *shapes):
        return pl.pallas_call(
            unpack_body,
            out_shape=[jax.ShapeDtypeStruct(s, f32) for s in shapes],
            compiler_params=pltpu.CompilerParams(vmem_limit_bytes=58 * 2**20),
            name="unpack",
        )(*halves)

    grad_gate, grad_up, grad_down = unpack(
        whole(feed_one_sum, feed_two_sum), (width, hidden), (width, hidden), (hidden, width)
    )
    grad_query, grad_key, grad_value, grad_out = unpack(
        whole(attention_one_sum, attention_two_sum), *([(width, width)] * 4)
    )
    return (
        section_output[None],
        input_grads[None],
        grad_attention_gain,
        grad_query[None],
        grad_key[None],
        grad_value[None],
        grad_out[None],
        grad_bias,
        grad_feed_gain,
        grad_gate[None],
        grad_up[None],
        grad_down[None],
    )


def solution(mesh):
    placed = (
        P(None, "dp", None),
        P(None, "dp"),
        P(None, "dp"),
        P(None, "dp"),
        P(None, "dp", None),
        P("section", None),
        P("section", None, None),
        P("section", None, None),
        P("section", None, None),
        P("section", None, None),
        P("section", None, None),
        P("section", None),
        P("section", None, None),
        P("section", None, None),
        P("section", None, None),
    )
    return jax.shard_map(
        per_device,
        mesh=mesh,
        in_specs=placed,
        out_specs=(
            P("section", None, "dp", None),
            P("section", None, "dp", None),
            P("section", None),
            P("section", None, None),
            P("section", None, None),
            P("section", None, None),
            P("section", None, None),
            P("section", None, None),
            P("section", None),
            P("section", None, None),
            P("section", None, None),
            P("section", None, None),
        ),
        check_vma=False,
    )
```

time: 785 us -> 393 us (0.50)
  matrix products: 300 us -> 0 us
  Pallas kernels: 0 us -> 161 us
  blocking collectives: 161 us -> 0 us
  local copies, waits for them, and re-layouts: 84.2 us -> 25.2 us
  starting transfers between devices: 22.6 us -> 69.4 us
  other arithmetic: 64.8 us -> 27.2 us
  waiting for transfers between devices: 126 us -> 101 us
  between operations: 20 us -> 1.84 us
    dot_general x190 -> x0, matrix products: 223 us -> none  [the longest x49 75.2 us: matmul_left(): lax.dot_general(left, right, (((0,), (0,)), ((), ())), preferred_element_...]
    pallas_call x0 -> x9, Pallas kernels: none -> 161 us  [the longest x2 58.9 us: attention_back(): call(functools.partial(attention_backward_body, layer), own_micro, [row_b...]
    psum x4 -> x0, blocking collectives: 161 us -> none  [the longest x1 44 us: standardize(): counts, series_totals = lax.psum((counts_here, totals_here), 'dp')]
    psum x1 -> x0, waiting for transfers between devices: 122 us -> none  [per_device(): lax.psum((feed_acc[0], feed_acc[1], feed_acc[2], feed_acc[3], attention_a...]
    ppermute x12 -> x52, waiting for transfers between devices: 3.67 us -> 101 us  [the longest x40 100 us: partner(): return lax.ppermute(x, ('section', 'dp'), pairs)]
    sub x7 -> x0, matrix products: 77.2 us -> none  [attention_backward(): softmax_grad - inner_sum]
    unnamed x880 -> x66, local copies, waits for them, and re-layouts: 75.5 us -> 10.5 us
    ppermute x12 -> x52, starting transfers between devices: 22.6 us -> 69.4 us  [the longest x40 67.6 us: partner(): return lax.ppermute(x, ('section', 'dp'), pairs)]
  transfers between devices with their start and end apart: 13 -> 52, of which waited for: 6 -> 33; matrix products, arithmetic and copies ran while one was open for 9% -> 12% of each run, Pallas kernels for 0% -> 11%
where the time goes in v1:
time: 393 us; the launch traced here: 385 us
  Pallas kernels  161 us (41%)
  waiting for transfers between devices  101 us (26%)
  starting transfers between devices  69.4 us (18%)
  other arithmetic  27.2 us (7%)
  local copies, waits for them, and re-layouts  25.2 us (6%)
    ppermute x40, waiting for transfers between devices, partner(): return lax.ppermute(x, ('section', 'dp'), pairs)  100 us
    ppermute x40, starting transfers between devices, partner(): return lax.ppermute(x, ('section', 'dp'), pairs)  67.6 us
    pallas_call x2, Pallas kernels, attention_back(): call(functools.partial(attention_backward_body, layer), own_micro, [row_b...  58.9 us
    pallas_call x1, Pallas kernels, per_device(): call(second_layer_body, own_micro, [SCALARS, row_block, by_batch((rows, w...  35.7 us
    pallas_call x1, Pallas kernels, per_device(): call(first_layer_body, own_micro, [SCALARS, by_batch((rows, width)), all_...  23.3 us
    pallas_call x1, Pallas kernels, per_device(): call(feed_backward_body, own_micro, [row_block, row_block, gain_spec] + w...  20.4 us
    unnamed x66, local copies, waits for them, and re-layouts  10.5 us
    pallas_call x1, Pallas kernels, per_device(): call(final_body, micro, [row_block, all_rows, by_step(stats_shape), by_st...  10.2 us
  transfers between devices with their start and end apart: 52, of which 33 were waited for; matrix products, arithmetic and copies ran while one was open for 12% of the time, Pallas kernels for 11%

profile of v1, /device:TPU:0, one launch (start us, length us, event | category | flops | bytes accessed | tf_op | source)
XLA Modules:
  0.0 385.4 jit_solution(15693116729137553575)
XLA Ops:
  0.7 6.0 %series_stats.1 = f32[6,8,128]{2,1,0:T(8,128)} custom-call(bf16[6,512,384]{2,1,0:T(8,128)(2,1)} %x_ref.5, s32[6,512]{1,0:T(8,128)} %sid_ref.9), custom_call_target="tpu_custom_call" | custom-call | tf_op jit(solution)/shard_map/series_stats/pallas_call | solution.py:667
  18.6 4.3 %fusion.4 = (f32[3,512,128]{2,1,0:T(8,128)}, f32[3,512,128]{2,1,0:T(8,128)}) fusion(f32[128]{0:T(128)S(1)} %get-tuple-element.140, f32[128]{0:T(128)S(1)} %get-tuple-element.141, f32[3,512]{1,0:T(4,128)S(1)} %fusion.7), kind=kLoop, calls=%fused_computation.23 | loop fusion | flops 393216 | bytes 1580032 | tf_op jit(solution)/shard_map/mul | solution.py:694
  33.3 23.3 %first_layer.1 = (bf16[3,512,384]{2,1,0:T(8,128)(2,1)}, f32[3,512,384]{2,1,0:T(8,128)}, bf16[3,512,1152]{2,1,0:T(8,128)(2,1)}, bf16[3,6,512,512]{3,2,1,0:T(8,128...) custom-call(s32[1]{0:T(128)} %bitcast.sec_ref, ...), custom_call_target="tpu_custom_call" | custom-call | flops 10871635968 | bytes 4194304 | tf_op jit(solution)/shard_map/first_layer/pallas_call | solution.py:732
  56.7 35.7 %second_layer.1 = (bf16[3,512,384]{2,1,0:T(8,128)(2,1)}, bf16[3,512,1152]{2,1,0:T(8,128)(2,1)}, bf16[3,6,512,512]{3,2,1,0:T(8,128)(2,1)}, f32[3,512,128]{2,1,0:T...) custom-call(s32[1]{0:T(128)} %bitcast.sec_ref, ...), custom_call_target="tpu_custom_call" | custom-call | flops 21743271936 | bytes 4194304 | tf_op jit(solution)/shard_map/second_layer/pallas_call | solution.py:743
  92.4 30.0 %attention_back_1.1 = (bf16[3,512,384]{2,1,0:T(8,128)(2,1)}, f32[3,8,128]{2,1,0:T(8,128)}, bf16[2,2304,128]{2,1,0:T(8,128)(2,1)}, f32[16,384]{1,0:T(8,128)}) custom-call(s32[1]{0:T(128)} %bitcast.sec_ref, f32[3,512,384]{2,1,0:T(8,128)} %get-tuple-element.48.middle_grad_ref, bf16[3,512,384]{2,1,0:T(8,128)(2,1)} %get-tuple-element.47.h_ref, ...), custom_call_target="tpu_custom_call" | custom-call | flops 10871635968 | bytes 4194304 | tf_op jit(solution)/shard_map/attention_back_1/pallas_call | solution.py:756
  122.4 20.4 %feed_back.1 = (f32[3,512,384]{2,1,0:T(8,128)}, bf16[2,4608,128]{2,1,0:T(8,128)(2,1)}, f32[8,384]{1,0:T(8,128)}) custom-call(s32[1]{0:T(128)} %bitcast.sec_ref, f32[3,512,384]{2,1,0:T(8,128)} %get-tuple-element.46.middle_ref, bf16[3,512,384]{2,1,0:T(8,128)(2,1)} %get-tuple-element.53.grad_ref.own_second, f32[8,384]{1,0:T(8,128)} %copy-done.18, ...), custom_call_target="tpu_custom_call" | custom-call | flops 10871635968 | bytes 4194304 | tf_op jit(solution)/shard_map/feed_back/pallas_call | solution.py:775
  145.3 28.9 %attention_back_0.1 = (f32[3,512,384]{2,1,0:T(8,128)}, f32[3,8,128]{2,1,0:T(8,128)}, bf16[2,2304,128]{2,1,0:T(8,128)(2,1)}, f32[16,384]{1,0:T(8,128)}) custom-call(s32[1]{0:T(128)} %bitcast.sec_ref, f32[3,512,384]{2,1,0:T(8,128)} %get-tuple-element.54.middle_grad_ref, f32[3,512,384]{2,1,0:T(8,128)} %get-tuple-element.55.h_ref, ...), custom_call_target="tpu_custom_call" | custom-call | flops 10871635968 | bytes 4194304 | tf_op jit(solution)/shard_map/attention_back_0/pallas_call | solution.py:756
  211.0 4.9 %collective-permute-done.15 = bf16[1152,128]{1,0:T(8,128)(2,1)S(1)} collective-permute-done((bf16[1152,128]{1,0:T(8,128)(2,1)S(1)}, bf16[1152,128]{1,0:T(8,128)(2,1)S(1)}, u32[]{:S(2)}, u32[]{:S(2)}) %collective-permute-start.15) | collective-permute-done | bytes 294944 | tf_op jit(solution)/shard_map/ppermute | solution.py:559
  216.6 6.1 %collective-permute-done.24 = bf16[1152,128]{1,0:T(8,128)(2,1)S(1)} collective-permute-done((bf16[1152,128]{1,0:T(8,128)(2,1)S(1)}, bf16[1152,128]{1,0:T(8,128)(2,1)S(1)}, u32[]{:S(2)}, u32[]{:S(2)}) %collective-permute-start.24) | collective-permute-done | bytes 294944 | tf_op jit(solution)/shard_map/ppermute | solution.py:559
  223.3 4.5 %collective-permute-done.16 = bf16[576,128]{1,0:T(8,128)(2,1)S(1)} collective-permute-done((bf16[576,128]{1,0:T(8,128)(2,1)S(1)}, bf16[576,128]{1,0:T(8,128)(2,1)S(1)}, u32[]{:S(2)}, u32[]{:S(2)}) %collective-permute-start.16) | collective-permute-done | bytes 147488 | tf_op jit(solution)/shard_map/ppermute | solution.py:559
  228.4 4.6 %collective-permute-done.25 = bf16[576,128]{1,0:T(8,128)(2,1)S(1)} collective-permute-done((bf16[576,128]{1,0:T(8,128)(2,1)S(1)}, bf16[576,128]{1,0:T(8,128)(2,1)S(1)}, u32[]{:S(2)}, u32[]{:S(2)}) %collective-permute-start.25) | collective-permute-done | bytes 147488 | tf_op jit(solution)/shard_map/ppermute | solution.py:559
  252.5 3.4 collective-permute-start.19
  270.6 4.9 %collective-permute-done.21 = bf16[576,128]{1,0:T(8,128)(2,1)S(1)} collective-permute-done((bf16[576,128]{1,0:T(8,128)(2,1)S(1)}, bf16[576,128]{1,0:T(8,128)(2,1)S(1)}, u32[]{:S(2)}, u32[]{:S(2)}) %collective-permute-start.21) | collective-permute-done | bytes 147488 | tf_op jit(solution)/shard_map/ppermute | solution.py:559
  276.8 3.8 collective-permute-done.30
  281.3 6.1 %collective-permute-done.22 = bf16[1152,128]{1,0:T(8,128)(2,1)S(1)} collective-permute-done((bf16[1152,128]{1,0:T(8,128)(2,1)S(1)}, bf16[1152,128]{1,0:T(8,128)(2,1)S(1)}, u32[]{:S(2)}, u32[]{:S(2)}) %collective-permute-start.22) | collective-permute-done | bytes 294944 | tf_op jit(solution)/shard_map/ppermute | solution.py:559
  288.0 6.1 %collective-permute-done.31 = bf16[1152,128]{1,0:T(8,128)(2,1)S(1)} collective-permute-done((bf16[1152,128]{1,0:T(8,128)(2,1)S(1)}, bf16[1152,128]{1,0:T(8,128)(2,1)S(1)}, u32[]{:S(2)}, u32[]{:S(2)}) %collective-permute-start.31) | collective-permute-done | bytes 294944 | tf_op jit(solution)/shard_map/ppermute | solution.py:559
  297.7 4.4 %collective-permute-done.35 = bf16[1152,128]{1,0:T(8,128)(2,1)S(1)} collective-permute-done((bf16[1152,128]{1,0:T(8,128)(2,1)S(1)}, bf16[1152,128]{1,0:T(8,128)(2,1)S(1)}, u32[]{:S(2)}, u32[]{:S(2)}) %collective-permute-start.35) | collective-permute-done | bytes 294944 | tf_op jit(solution)/shard_map/ppermute | solution.py:559
  302.3 4.5 %collective-permute-start.36 = (bf16[576,128]{1,0:T(8,128)(2,1)S(1)}, bf16[576,128]{1,0:T(8,128)(2,1)S(1)}, u32[]{:S(2)}, u32[]{:S(2)}) collective-permute-start(bf16[576,128]{1,0:T(8,128)(2,1)S(1)} %constant_dynamic-slice_fusion.5), channel_id=1, source_target_pairs={{0,4},{1,5},{2,6},{3,7},{4,0},{5,1},{6,2},{7,3},{8,12},{9,13},{10,... | collective-permute-start | bytes 442376 | tf_op jit(solution)/shard_map/ppermute | solution.py:559
  323.8 5.5 %collective-permute-done.47 = bf16[288,128]{1,0:T(8,128)(2,1)S(1)} collective-permute-done((bf16[288,128]{1,0:T(8,128)(2,1)S(1)}, bf16[288,128]{1,0:T(8,128)(2,1)S(1)}, u32[]{:S(2)}, u32[]{:S(2)}) %collective-permute-start.47) | collective-permute-done | bytes 73760 | tf_op jit(solution)/shard_map/ppermute | solution.py:559
  329.6 3.7 collective-permute-start.40
  341.6 3.6 collective-permute-done.49
  349.7 6.1 %collective-permute-done.50 = bf16[2304,128]{1,0:T(8,128)(2,1)S(1)} collective-permute-done((bf16[2304,128]{1,0:T(8,128)(2,1)S(1)}, bf16[2304,128]{1,0:T(8,128)(2,1)S(1)}, u32[]{:S(2)}, u32[]{:S(2)}) %collective-permute-start.50) | collective-permute-done | bytes 589856 | tf_op jit(solution)/shard_map/ppermute | solution.py:559
  362.4 10.2 %final.1 = (f32[6,512,384]{2,1,0:T(8,128)}, bf16[6,512,384]{2,1,0:T(8,128)(2,1)}) custom-call(s32[1]{0:T(128)} %bitcast.sec_ref, bf16[6,512,384]{2,1,0:T(8,128)(2,1)} %x_ref.5, s32[6,512]{1,0:T(8,128)} %sid_ref.9, f32[6,8,128]{2,1,0:T(8,128)} %maximum_maximum_fusion.3.stats_ref, f32[6,8,128]{2,1,0:T(8,128)} %slice_bitcast_fusion.4.series_ref, ...), custom_call_target="tpu_custom_call" | custom-call | flops 100000000 | bytes 4194304 | tf_op jit(solution)/shard_map/final/pallas_call | solution.py:829
  381.0 4.0 %unpack.3 = (f32[384,1024]{1,0:T(8,128)}, f32[384,1024]{1,0:T(8,128)}, f32[1024,384]{1,0:T(8,128)}) custom-call(bf16[4608,128]{1,0:T(8,128)(2,1)} %get-tuple-element.87.low_ref, bf16[4608,128]{1,0:T(8,128)(2,1)} %get-tuple-element.86.high_ref), custom_call_target="tpu_custom_call" | custom-call | tf_op jit(solution)/shard_map/unpack/pallas_call | solution.py:845
  (268 shorter events, 148.4 us)
Async XLA Ops:
  6.7 9.4 %collective-permute-start = (f32[6,8,128]{2,1,0:T(8,128)}, f32[6,8,128]{2,1,0:T(8,128)S(1)}, u32[]{:S(2)}, u32[]{:S(2)}) collective-permute-start(f32[6,8,128]{2,1,0:T(8,128)} %series_stats.1), channel_id=1, source_target_pairs={{0,1},{1,0},{2,3},{3,2},{4,5},{5,4},{6,7},{7,6},{8,9},{9,8},{10,11... | collective-permute-start | bytes 73736 | tf_op jit(solution)/shard_map/ppermute | solution.py:559
  9.9 14.8 %collective-permute-start.4 = (f32[8,384]{1,0:T(8,128)S(1)}, f32[8,384]{1,0:T(8,128)S(1)}, u32[]{:S(2)}, u32[]{:S(2)}) collective-permute-start(f32[8,384]{1,0:T(8,128)S(1)} %pad_convert_fusion), channel_id=1, source_target_pairs={{0,16},{16,0},{1,17},{17,1},{2,18},{18,2},{3,19},{19,3},{4,20},{20... | collective-permute-start | bytes 36872 | tf_op jit(solution)/shard_map/ppermute | solution.py:540
  15.0 17.4 %collective-permute-start.5 = (bf16[384,3584]{1,0:T(8,128)(2,1)}, bf16[384,3584]{1,0:T(8,128)(2,1)}, u32[]{:S(2)}, u32[]{:S(2)}) collective-permute-start(bf16[384,3584]{1,0:T(8,128)(2,1)} %bitcast_dynamic-update-slice_fusion.own_big), channel_id=1, source_target_pairs={{0,16},{16,0},{1,17},{17,1},{2,18},{18,2},{3,19},{19,3},{4,20},{20... | collective-permute-start | bytes 8257544 | tf_op jit(solution)/shard_map/ppermute | solution.py:540
  15.5 16.9 %collective-permute-start.6 = (bf16[1024,384]{1,0:T(8,128)(2,1)S(1)}, bf16[1024,384]{1,0:T(8,128)(2,1)S(1)}, u32[]{:S(2)}, u32[]{:S(2)}) collective-permute-start(bf16[1024,384]{1,0:T(8,128)(2,1)S(1)} %bitcast.77), channel_id=1, source_target_pairs={{0,16},{16,0},{1,17},{17,1},{2,18},{18,2},{3,19},{19,3},{4,20},{20... | collective-permute-start | bytes 2359304 | tf_op jit(solution)/shard_map/ppermute | solution.py:540
  145.3 110.7 %collective-permute-start.33 = (bf16[4608,128]{1,0:T(8,128)(2,1)}, bf16[4608,128]{1,0:T(8,128)(2,1)S(1)}, u32[]{:S(2)}, u32[]{:S(2)}) collective-permute-start(bf16[4608,128]{1,0:T(8,128)(2,1)} %slice_bitcast_fusion.1), channel_id=1, source_target_pairs={{0,16},{16,0},{1,17},{17,1},{2,18},{18,2},{3,19},{19,3},{4,20},{20... | collective-permute-start | bytes 3538952 | tf_op jit(solution)/shard_map/ppermute | solution.py:540
  184.0 72.4 %collective-permute-start.42 = (bf16[4608,128]{1,0:T(8,128)(2,1)}, bf16[4608,128]{1,0:T(8,128)(2,1)S(1)}, u32[]{:S(2)}, u32[]{:S(2)}) collective-permute-start(bf16[4608,128]{1,0:T(8,128)(2,1)} %slice_bitcast_fusion), channel_id=1, source_target_pairs={{0,16},{16,0},{1,17},{17,1},{2,18},{18,2},{3,19},{19,3},{4,20},{20... | collective-permute-start | bytes 3538952 | tf_op jit(solution)/shard_map/ppermute | solution.py:540
  189.0 18.7 %collective-permute-start.14 = (bf16[2304,128]{1,0:T(8,128)(2,1)}, bf16[2304,128]{1,0:T(8,128)(2,1)}, u32[]{:S(2)}, u32[]{:S(2)}) collective-permute-start(bf16[2304,128]{1,0:T(8,128)(2,1)} %slice_bitcast_fusion.3), channel_id=1, source_target_pairs={{0,16},{16,0},{1,17},{17,1},{2,18},{18,2},{3,19},{19,3},{4,20},{20... | collective-permute-start | bytes 1769480 | tf_op jit(solution)/shard_map/ppermute | solution.py:540
  194.8 14.4 %collective-permute-start.23 = (bf16[2304,128]{1,0:T(8,128)(2,1)}, bf16[2304,128]{1,0:T(8,128)(2,1)}, u32[]{:S(2)}, u32[]{:S(2)}) collective-permute-start(bf16[2304,128]{1,0:T(8,128)(2,1)} %slice_bitcast_fusion.2), channel_id=1, source_target_pairs={{0,16},{16,0},{1,17},{17,1},{2,18},{18,2},{3,19},{19,3},{4,20},{20... | collective-permute-start | bytes 1769480 | tf_op jit(solution)/shard_map/ppermute | solution.py:540
  204.0 158.5 %collective-permute-start.13 = (bf16[3,512,384]{2,1,0:T(8,128)(2,1)}, bf16[3,512,384]{2,1,0:T(8,128)(2,1)}, u32[]{:S(2)}, u32[]{:S(2)}) collective-permute-start(bf16[3,512,384]{2,1,0:T(8,128)(2,1)} %get-tuple-element.88), channel_id=1, source_target_pairs={{0,16},{16,0},{1,17},{17,1},{2,18},{18,2},{3,19},{19,3},{4,20},{20... | collective-permute-start | bytes 3538952 | tf_op jit(solution)/shard_map/ppermute | solution.py:540
  207.7 154.7 %collective-permute-start.12 = (bf16[3,512,384]{2,1,0:T(8,128)(2,1)}, bf16[3,512,384]{2,1,0:T(8,128)(2,1)}, u32[]{:S(2)}, u32[]{:S(2)}) collective-permute-start(bf16[3,512,384]{2,1,0:T(8,128)(2,1)} %convert_select_fusion), channel_id=1, source_target_pairs={{0,16},{16,0},{1,17},{17,1},{2,18},{18,2},{3,19},{19,3},{4,20},{20... | collective-permute-start | bytes 3538952 | tf_op jit(solution)/shard_map/ppermute | solution.py:540
  209.2 6.8 %collective-permute-start.15 = (bf16[1152,128]{1,0:T(8,128)(2,1)S(1)}, bf16[1152,128]{1,0:T(8,128)(2,1)S(1)}, u32[]{:S(2)}, u32[]{:S(2)}) collective-permute-start(bf16[1152,128]{1,0:T(8,128)(2,1)S(1)} %constant_dynamic-slice_fusion.15), channel_id=1, source_target_pairs={{0,1},{1,0},{2,3},{3,2},{4,5},{5,4},{6,7},{7,6},{8,9},{9,8},{10,11... | collective-permute-start | bytes 884744 | tf_op jit(solution)/shard_map/ppermute | solution.py:559
  256.4 38.8 %collective-permute-start.34 = (bf16[2304,128]{1,0:T(8,128)(2,1)S(1)}, bf16[2304,128]{1,0:T(8,128)(2,1)S(1)}, u32[]{:S(2)}, u32[]{:S(2)}) collective-permute-start(bf16[2304,128]{1,0:T(8,128)(2,1)S(1)} %constant_dynamic-slice_fusion.7), channel_id=1, source_target_pairs={{0,1},{1,0},{2,3},{3,2},{4,5},{5,4},{6,7},{7,6},{8,9},{9,8},{10,11... | collective-permute-start | bytes 1769480 | tf_op jit(solution)/shard_map/ppermute | solution.py:559
  258.1 39.2 %collective-permute-start.43 = (bf16[2304,128]{1,0:T(8,128)(2,1)S(1)}, bf16[2304,128]{1,0:T(8,128)(2,1)S(1)}, u32[]{:S(2)}, u32[]{:S(2)}) collective-permute-start(bf16[2304,128]{1,0:T(8,128)(2,1)S(1)} %constant_dynamic-slice_fusion.3), channel_id=1, source_target_pairs={{0,1},{1,0},{2,3},{3,2},{4,5},{5,4},{6,7},{7,6},{8,9},{9,8},{10,11... | collective-permute-start | bytes 1769480 | tf_op jit(solution)/shard_map/ppermute | solution.py:559
  295.2 77.5 %collective-permute-start.32 = (bf16[2304,128]{1,0:T(8,128)(2,1)}, bf16[2304,128]{1,0:T(8,128)(2,1)}, u32[]{:S(2)}, u32[]{:S(2)}) collective-permute-start(bf16[2304,128]{1,0:T(8,128)(2,1)} %broadcast_select_fusion.12), channel_id=1, source_target_pairs={{0,16},{16,0},{1,17},{17,1},{2,18},{18,2},{3,19},{19,3},{4,20},{20... | collective-permute-start | bytes 1769480 | tf_op jit(solution)/shard_map/ppermute | solution.py:540
  297.4 9.4 %collective-permute-start.44 = (bf16[1152,128]{1,0:T(8,128)(2,1)S(1)}, bf16[1152,128]{1,0:T(8,128)(2,1)S(1)}, u32[]{:S(2)}, u32[]{:S(2)}) collective-permute-start(bf16[1152,128]{1,0:T(8,128)(2,1)S(1)} %constant_dynamic-slice_fusion.2), channel_id=1, source_target_pairs={{0,2},{1,3},{2,0},{3,1},{4,6},{5,7},{6,4},{7,5},{8,10},{9,11},{10,... | collective-permute-start | bytes 884744 | tf_op jit(solution)/shard_map/ppermute | solution.py:559
  302.3 7.9 %collective-permute-start.36 = (bf16[576,128]{1,0:T(8,128)(2,1)S(1)}, bf16[576,128]{1,0:T(8,128)(2,1)S(1)}, u32[]{:S(2)}, u32[]{:S(2)}) collective-permute-start(bf16[576,128]{1,0:T(8,128)(2,1)S(1)} %constant_dynamic-slice_fusion.5), channel_id=1, source_target_pairs={{0,4},{1,5},{2,6},{3,7},{4,0},{5,1},{6,2},{7,3},{8,12},{9,13},{10,... | collective-permute-start | bytes 442376 | tf_op jit(solution)/shard_map/ppermute | solution.py:559
  306.9 6.9 %collective-permute-start.45 = (bf16[576,128]{1,0:T(8,128)(2,1)S(1)}, bf16[576,128]{1,0:T(8,128)(2,1)S(1)}, u32[]{:S(2)}, u32[]{:S(2)}) collective-permute-start(bf16[576,128]{1,0:T(8,128)(2,1)S(1)} %constant_dynamic-slice_fusion.1), channel_id=1, source_target_pairs={{0,4},{1,5},{2,6},{3,7},{4,0},{5,1},{6,2},{7,3},{8,12},{9,13},{10,... | collective-permute-start | bytes 442376 | tf_op jit(solution)/shard_map/ppermute | solution.py:559
  319.3 10.0 %collective-permute-start.47 = (bf16[288,128]{1,0:T(8,128)(2,1)S(1)}, bf16[288,128]{1,0:T(8,128)(2,1)S(1)}, u32[]{:S(2)}, u32[]{:S(2)}) collective-permute-start(bf16[288,128]{1,0:T(8,128)(2,1)S(1)} %add_convert_fusion.10), channel_id=1, source_target_pairs={{0,8},{1,9},{2,10},{3,11},{4,12},{5,13},{6,14},{7,15},{8,0},{9,1},... | collective-permute-start | bytes 221192 | tf_op jit(solution)/shard_map/ppermute | solution.py:559
  321.8 7.6 %collective-permute-start.39 = (bf16[576,128]{1,0:T(8,128)(2,1)S(1)}, bf16[576,128]{1,0:T(8,128)(2,1)S(1)}, u32[]{:S(2)}, u32[]{:S(2)}) collective-permute-start(bf16[576,128]{1,0:T(8,128)(2,1)S(1)} %pad_maximum_fusion.12), channel_id=1, source_target_pairs={{0,4},{1,5},{2,6},{3,7},{4,0},{5,1},{6,2},{7,3},{8,12},{9,13},{10,... | collective-permute-start | bytes 442376 | tf_op jit(solution)/shard_map/ppermute | solution.py:559
  329.6 9.3 %collective-permute-start.40 = (bf16[1152,128]{1,0:T(8,128)(2,1)S(1)}, bf16[1152,128]{1,0:T(8,128)(2,1)S(1)}, u32[]{:S(2)}, u32[]{:S(2)}) collective-permute-start(bf16[1152,128]{1,0:T(8,128)(2,1)S(1)} %pad_maximum_fusion.8), channel_id=1, source_target_pairs={{0,2},{1,3},{2,0},{3,1},{4,6},{5,7},{6,4},{7,5},{8,10},{9,11},{10,... | collective-permute-start | bytes 884744 | tf_op jit(solution)/shard_map/ppermute | solution.py:559
  334.7 10.5 %collective-permute-start.49 = (bf16[1152,128]{1,0:T(8,128)(2,1)S(1)}, bf16[1152,128]{1,0:T(8,128)(2,1)S(1)}, u32[]{:S(2)}, u32[]{:S(2)}) collective-permute-start(bf16[1152,128]{1,0:T(8,128)(2,1)S(1)} %pad_maximum_fusion.9), channel_id=1, source_target_pairs={{0,2},{1,3},{2,0},{3,1},{4,6},{5,7},{6,4},{7,5},{8,10},{9,11},{10,... | collective-permute-start | bytes 884744 | tf_op jit(solution)/shard_map/ppermute | solution.py:559
  339.1 10.4 %collective-permute-start.41 = (bf16[2304,128]{1,0:T(8,128)(2,1)S(1)}, bf16[2304,128]{1,0:T(8,128)(2,1)S(1)}, u32[]{:S(2)}, u32[]{:S(2)}) collective-permute-start(bf16[2304,128]{1,0:T(8,128)(2,1)S(1)} %pad_maximum_fusion.4), channel_id=1, source_target_pairs={{0,1},{1,0},{2,3},{3,2},{4,5},{5,4},{6,7},{7,6},{8,9},{9,8},{10,11... | collective-permute-start | bytes 1769480 | tf_op jit(solution)/shard_map/ppermute | solution.py:559
  345.4 10.4 %collective-permute-start.50 = (bf16[2304,128]{1,0:T(8,128)(2,1)S(1)}, bf16[2304,128]{1,0:T(8,128)(2,1)S(1)}, u32[]{:S(2)}, u32[]{:S(2)}) collective-permute-start(bf16[2304,128]{1,0:T(8,128)(2,1)S(1)} %pad_maximum_fusion.5), channel_id=1, source_target_pairs={{0,1},{1,0},{2,3},{3,2},{4,5},{5,4},{6,7},{7,6},{8,9},{9,8},{10,11... | collective-permute-start | bytes 1769480 | tf_op jit(solution)/shard_map/ppermute | solution.py:559
  357.3 20.4 %collective-permute-start.51 = (bf16[4608,128]{1,0:T(8,128)(2,1)}, bf16[4608,128]{1,0:T(8,128)(2,1)}, u32[]{:S(2)}, u32[]{:S(2)}) collective-permute-start(bf16[4608,128]{1,0:T(8,128)(2,1)} %broadcast_select_fusion.2), channel_id=1, source_target_pairs={{0,16},{16,0},{1,17},{17,1},{2,18},{18,2},{3,19},{19,3},{4,20},{20... | collective-permute-start | bytes 3538952 | tf_op jit(solution)/shard_map/ppermute | solution.py:540
  (55 other events, 407.2 us)
